TPU v7x, 32 devices: a whole 2x2x4 slice. The times are simulated.
32 devices in a mesh: row: 4 (over y, x), grp: 8 (over z, core).
Axes of the slice: x: 2, y: 2, z: 4, core: 2. Of those that a mesh axis runs over, the one named last changes fastest.
Arguments:
- segments: bfloat16 [8, 64, 128, 512], P('grp', 'row'), may hold values from -40 to 40
- conv_weight: bfloat16 [3, 512, 512], replicated, may hold values from -0.15625 to 0.15625
- gain: float32 [512], replicated, may hold values from 0.1 to 1.9
- head: bfloat16 [512, 128], replicated, may hold values from -0.25 to 0.25
- group: int32 [8, 64], P('grp', 'row'), may hold values from 0 to 7
- positive: int32 [8, 64], P('grp', 'row'), may hold values from 0 to 63, as said below
Outputs:
- grad_conv: float32 [3, 512, 512], replicated
- grad_gain: float32 [512], replicated
- projector_derivative: float32 [512, 128], replicated
Inputs may be any that keep to these rules, and one draw needn't show every extreme that they name: positive[c, i] is another segment of the same index c with the same group, and positive[c, positive[c, i]] == i.
All inputs are finite; a program needn't handle non-finite values.
Results may differ from a plain program's by a relative error of at most 0.003.
The roundings to bfloat16 on the way count: a program that leaves them out, or rounds other values in their place, can miss the bound.
Values sent between devices are 32-bit elements; how exact they have to be, the bound alone decides.
A program may use at most 64 MiB of HBM per device.

v0:
```python
from functools import partial

import jax
import jax.numpy as jnp
from jax import lax
from jax.sharding import PartitionSpec as P

DILATION_GAP = 2


logit_divisor = 0.1


def unit_rows(values):
    return values * lax.rsqrt(jnp.mean(values * values, axis=-1, keepdims=True) + 1e-05)


def scale_embed(projected):
    return unit_rows(projected) * projected.shape[-1] ** (-0.5)


def filter_tap_window(normalized_rows, filter_tap_index, spacing):
    sequence_length = normalized_rows.shape[1]
    padded = jnp.pad(normalized_rows, ((0, 0), (spacing, spacing), (0, 0)))
    return padded[:, filter_tap_index * spacing : filter_tap_index * spacing + sequence_length]


def reverse_tap_gather(term, filter_tap_index, spacing):
    sequence_length = term.shape[1]
    padded = jnp.pad(term, ((0, 0), (spacing, spacing), (0, 0)))
    begin = (2 - filter_tap_index) * spacing
    return padded[:, begin : begin + sequence_length]


def encode(patient_piece_records, conv_weight, gain, head):
    inputs = patient_piece_records.astype(jnp.float32)
    unit = unit_rows(inputs)
    normalized_rows = (unit * gain).astype(jnp.bfloat16)
    segment_count, sequence_length, channel_count = normalized_rows.shape
    conv = jnp.zeros((segment_count * sequence_length, channel_count), jnp.float32)
    for filter_tap_index in range(conv_weight.shape[0]):
        shifted_input = filter_tap_window(normalized_rows, filter_tap_index, DILATION_GAP).reshape(
            segment_count * sequence_length, channel_count
        )
        conv = conv + jnp.dot(
            shifted_input, conv_weight[filter_tap_index], preferred_element_type=jnp.float32
        )
    conv = conv.reshape(segment_count, sequence_length, channel_count)
    hidden = inputs + jax.nn.gelu(conv, approximate=True)
    pooled = jnp.mean(hidden, axis=1).astype(jnp.bfloat16)
    projected = jnp.dot(pooled, head, preferred_element_type=jnp.float32)
    return (unit, normalized_rows, conv, pooled, projected)


def backward(embed_grad, unit, normalized_rows, conv, pooled, projected, conv_weight, head):
    projected_grad = jax.vjp(scale_embed, projected)[1](embed_grad)[0]
    projector_derivative = jnp.dot(
        pooled.astype(jnp.float32).T, projected_grad, precision=lax.Precision.HIGHEST
    )
    pooled_grad = jnp.dot(
        projected_grad, head.astype(jnp.float32).T, precision=lax.Precision.HIGHEST
    )
    segment_count, sequence_length, channel_count = conv.shape
    hidden_grad = jnp.broadcast_to(pooled_grad[:, None, :] / sequence_length, conv.shape)
    conv_grad = jax.vjp(partial(jax.nn.gelu, approximate=True), conv)[1](hidden_grad)[0].astype(
        jnp.bfloat16
    )
    flat_grad = conv_grad.reshape(segment_count * sequence_length, channel_count)
    tap_grads = []
    normalized_gradient = jnp.zeros((segment_count, sequence_length, channel_count), jnp.float32)
    for filter_tap_index in range(conv_weight.shape[0]):
        shifted_input = filter_tap_window(normalized_rows, filter_tap_index, DILATION_GAP).reshape(
            segment_count * sequence_length, channel_count
        )
        tap_grads.append(
            lax.dot_general(
                shifted_input,
                flat_grad,
                (((0,), (0,)), ((), ())),
                preferred_element_type=jnp.float32,
            )
        )
        backward_term = lax.dot_general(
            flat_grad,
            conv_weight[filter_tap_index],
            (((1,), (1,)), ((), ())),
            preferred_element_type=jnp.float32,
        )
        normalized_gradient = normalized_gradient + reverse_tap_gather(
            backward_term.reshape(segment_count, sequence_length, channel_count),
            filter_tap_index,
            DILATION_GAP,
        )
    grad_conv = jnp.stack(tap_grads)
    grad_gain = jnp.sum(normalized_gradient * unit, axis=(0, 1))
    return (grad_conv, grad_gain, projector_derivative)


def body(segments, conv_weight, gain, head, group, positive):
    patient_piece_records = segments[0]
    group_ids = group[0]
    partners = positive[0]
    unit, normalized_rows, conv, pooled, projected = encode(
        patient_piece_records, conv_weight, gain, head
    )
    encounter_latent_vector = scale_embed(projected)
    gathered_embedding, all_groups = (
        lax.all_gather(encounter_latent_vector, "row", axis=0, tiled=True),
        lax.all_gather(group_ids, "row", axis=0, tiled=True),
    )
    local_count = encounter_latent_vector.shape[0]
    matrix_height_number = gathered_embedding.shape[0]
    global_multiplier = (matrix_height_number * lax.axis_size("grp")) ** (-0.5) / logit_divisor
    own_rows = lax.axis_index("row") * local_count + jnp.arange(local_count, dtype=jnp.int32)
    columns = jnp.arange(matrix_height_number, dtype=jnp.int32)
    cosine_affinity_matrix = (
        jnp.dot(encounter_latent_vector, gathered_embedding.T, precision=lax.Precision.HIGHEST)
        / logit_divisor
    )
    same_group = (group_ids[:, None] == all_groups[None, :]) & (
        own_rows[:, None] != columns[None, :]
    )
    log_total = jnp.log(
        jnp.sum(jnp.where(same_group, jnp.exp(cosine_affinity_matrix), 0.0), axis=1)
    )
    softmax = jnp.where(same_group, jnp.exp(cosine_affinity_matrix - log_total[:, None]), 0.0)
    row_term = jnp.dot(softmax, gathered_embedding, precision=lax.Precision.HIGHEST)
    partner_pick = (partners[:, None] == columns[None, :]).astype(jnp.float32)
    partner_embed = jnp.dot(partner_pick, gathered_embedding, precision=lax.Precision.HIGHEST)
    all_totals = lax.all_gather(log_total, "row", axis=0, tiled=True)
    transposed = jnp.where(same_group, jnp.exp(cosine_affinity_matrix - all_totals[None, :]), 0.0)
    column_term = jnp.dot(transposed, gathered_embedding, precision=lax.Precision.HIGHEST)
    embed_grad = global_multiplier * (row_term + column_term - 2.0 * partner_embed)
    grads = backward(embed_grad, unit, normalized_rows, conv, pooled, projected, conv_weight, head)
    grads = lax.psum((grads[0], grads[1], grads[2]), ("row", "grp"))
    return (grads[0], grads[1], grads[2])


def solution(mesh):
    placed = (P("grp", "row", None, None), P(), P(), P(), P("grp", "row"), P("grp", "row"))
    return jax.shard_map(
        body, mesh=mesh, in_specs=placed, out_specs=(P(), P(), P()), check_vma=False
    )
```

profile of v0, /device:TPU:0, one launch (start us, length us, event | category | flops | bytes accessed | tf_op | source)
XLA Modules:
  0.0 249.4 jit_solution(9741512662416394120)
XLA Ops:
  7.2 0.0 copy-start
  7.2 0.0 copy-start.10
  7.2 0.0 all-reduce.8.cloned.1.call-start
  7.2 3.0 %copy.23 = bf16[1,16,128,512]{2,3,1,0:T(8,128)(2,1)S(1)} copy(bf16[1,16,128,512]{3,2,1,0:T(8,128)(2,1)} %param.6) | data formatting | bytes 4194304 | tf_op args[0]
  10.3 0.4 fusion.7
  10.7 0.0 copy-done.10
  10.7 0.7 fusion.5
  11.4 0.0 copy-start.5
  11.4 2.1 fusion.10
  13.5 3.2 %pad_slice_fusion.2 = (bf16[16,128,512]{1,2,0:T(8,128)(2,1)}, bf16[16,128,512]{1,2,0:T(8,128)(2,1)}) fusion(bf16[16,128,512]{1,2,0:T(8,128)(2,1)S(1)} %fusion.5), kind=kLoop, calls=%fused_computation.13 | loop fusion | bytes 6291456 | tf_op jit(solution)/shard_map/slice | solution.py:25
  16.7 0.0 copy-done.5
  16.7 3.9 %copy.24 = bf16[16,128,512]{2,1,0:T(8,128)(2,1)} copy(bf16[16,128,512]{1,2,0:T(8,128)(2,1)} %get-tuple-element.6) | data formatting | bytes 4194304 | tf_op jit(solution)/shard_map/slice | solution.py:25
  20.6 3.9 %copy.25 = bf16[1,16,128,512]{3,2,1,0:T(8,128)(2,1)} copy(bf16[1,16,128,512]{2,3,1,0:T(8,128)(2,1)} %fusion.10) | data formatting | bytes 4194304 | tf_op jit(solution)/shard_map/convert_element_type | solution.py:38
  24.6 5.0 %fusion.45 = f32[2048,512]{1,0:T(8,128)} fusion(bf16[2048,512]{1,0:T(8,128)(2,1)} %bitcast.96, bf16[3,512,512]{2,1,0:T(8,128)(2,1)} %param.7), kind=kOutput, calls=%fused_computation.63 | convolution fusion | flops 1073741824 | bytes 6815744 | tf_op jit(solution)/shard_map/dot_general | solution.py:45
  29.6 0.0 copy-done.4
  29.6 4.3 %fusion.43 = f32[2048,512]{1,0:T(8,128)} fusion(bf16[2048,512]{1,0:T(8,128)(2,1)S(1)} %bitcast.97, bf16[3,512,512]{2,1,0:T(8,128)(2,1)} %param.7), kind=kOutput, calls=%fused_computation.61 | convolution fusion | flops 1073741824 | bytes 6815744 | tf_op jit(solution)/shard_map/dot_general | solution.py:45
  33.9 3.9 %copy.26 = bf16[16,128,512]{2,1,0:T(8,128)(2,1)} copy(bf16[16,128,512]{1,2,0:T(8,128)(2,1)} %get-tuple-element.5) | data formatting | bytes 4194304 | tf_op jit(solution)/shard_map/slice | solution.py:25
  37.8 7.4 %add_add_fusion = f32[2048,512]{1,0:T(8,128)} fusion(f32[2048,512]{1,0:T(8,128)} %fusion.45, f32[2048,512]{1,0:T(8,128)} %fusion.43, bf16[2048,512]{1,0:T(8,128)(2,1)} %bitcast.98, bf16[3,512,512]{2,1,0:T(8,128)(2,1)} %param.7), kind=kOutput, calls=%fused_computation.44 | convolution fusion | flops 1075838976 | bytes 15204352 | tf_op jit(solution)/shard_map/dot_general | solution.py:45
  45.2 5.3 %copy.30 = f32[16,128,512]{1,2,0:T(8,128)} copy(f32[16,128,512]{2,1,0:T(8,128)} %bitcast.91) | data formatting | bytes 8388608 | tf_op jit(solution)/shard_map/reshape | solution.py:48
  50.5 3.4 %fusion.8 = f32[16,512]{1,0:T(8,128)S(1)} fusion(bf16[1,16,128,512]{2,3,1,0:T(8,128)(2,1)S(1)} %copy.23, f32[16,128,512]{1,2,0:T(8,128)} %copy.30), kind=kLoop, calls=%fused_computation.18 | loop fusion | flops 11526144 | bytes 6324224 | tf_op jit(solution)/shard_map/reduce_sum | solution.py:50
  53.9 0.0 copy-done
  54.0 0.2 multiply_reduce_fusion.1
  54.2 0.1 multiply_multiply_fusion.4
  54.3 9.6 %all_gather.10 = f32[64,128]{1,0:T(8,128)S(1)} all-gather(f32[16,128]{1,0:T(8,128)S(1)} %multiply_multiply_fusion.4), channel_id=1, replica_groups=mesh['row'=4,'grp'=8] {'row'}, dimensions={0}, use_global_device_ids=true | all-gather | bytes 40960 | tf_op jit(solution)/shard_map/all_gather | solution.py:108
  63.9 0.0 copy-done.13
  63.9 0.6 dynamic-slice
  65.2 0.0 copy-done.11
  65.2 0.1 bitcast_dynamic-update-slice_fusion
  65.3 7.4 %all-reduce.3 = s32[64]{0:T(128)S(1)} all-reduce(s32[64]{0:T(128)S(1)} %bitcast_dynamic-update-slice_fusion), channel_id=2, replica_groups=mesh['row'=4,'grp'=8] {'row'}, use_global_device_ids=true, to_apply=%add.3 | all-reduce | flops 64 | bytes 512
  72.6 0.3 select_reduce_fusion
  72.9 0.1 log_dynamic-update-slice_fusion
  73.0 9.1 %all-reduce.4 = f32[64]{0:T(128)S(1)} all-reduce(f32[64]{0:T(128)S(1)} %get-tuple-element.11), channel_id=1, replica_groups=mesh['row'=4,'grp'=8] {'row'}, use_global_device_ids=true, to_apply=%add.4 | all-reduce | flops 64 | bytes 512
  82.1 0.2 fusion.56
  82.3 0.2 convolution_add_fusion
  82.5 0.0 copy-done.12
  82.5 0.3 multiply_reduce_fusion
  82.9 0.3 broadcast_multiply_fusion
  83.1 6.7 %fusion.17 = bf16[16,128,512]{1,2,0:T(8,128)(2,1)S(1)} fusion(f32[16,128,512]{1,2,0:T(8,128)} %copy.30, f32[16,512]{1,0:T(8,128)S(1)} %get-tuple-element.8, f32[16,512]{1,0:T(8,128)S(1)} %get-tuple-element.7), kind=kLoop, calls=%fused_computation.27 | loop fusion | flops 19922944 | bytes 6356992 | tf_op jit(solution)/shard_map/convert_element_type | solution.py:65
  89.8 0.0 copy-done.1
  89.8 0.0 copy-start.6
  89.8 2.7 %fusion.24 = bf16[2048,512]{1,0:T(8,128)(2,1)S(1)} fusion(f32[2048,512]{1,0:T(8,128)S(1)} %copy-done.1, f32[16,512]{1,0:T(8,128)S(1)} %get-tuple-element.8, f32[16,512]{1,0:T(8,128)S(1)} %get-tuple-element.7), kind=kLoop, calls=%fused_computation.34 | loop fusion | flops 19922944 | bytes 6356992 | tf_op jit(solution)/shard_map/convert_element_type | solution.py:65
  92.5 0.0 copy-done.6
  92.5 0.0 copy-start.2
  92.6 1.3 convolution_bitcast_fusion
  93.9 0.0 copy-start.7
  93.9 1.3 convolution_bitcast_fusion.1
  95.2 1.0 fusion.61
  96.2 0.0 copy-done.2
  96.2 0.0 copy-done.7
  96.2 1.2 fusion.33
  97.5 2.0 pad_maximum_fusion
  99.4 0.0 all-reduce.8.cloned.1.call-update
  99.5 0.0 copy-start.3
  99.5 0.0 copy-start.8
  99.5 3.1 %fusion.40 = f32[16,128,512]{1,2,0:T(8,128)S(1)} fusion(bf16[16,128,512]{2,1,0:T(8,128)(2,1)} %bitcast.93, bf16[3,512,512]{2,1,0:T(8,128)(2,1)} %param.7), kind=kOutput, calls=%fused_computation.58 | convolution fusion | flops 1073741824 | bytes 6815744 | tf_op jit(solution)/shard_map/dot_general | solution.py:83
  102.6 0.0 copy-done.3
  102.6 0.0 copy-done.8
  102.6 1.3 fusion.37
  103.9 2.6 %fusion.6 = f32[512]{0:T(512)S(1)} fusion(bf16[1,16,128,512]{2,3,1,0:T(8,128)(2,1)S(1)} %copy.23, f32[16,128,512]{1,2,0:T(8,128)S(1)} %fusion.40, f32[16,128,512]{1,2,0:T(8,128)S(1)} %fusion.37, bf16[16,128,512]{2,1,0:T(8,128)(2,1)S(1)} %bitcast.95, f32[16,128]{1,0:T(8,128)S(1)} %add_rsqrt_fusion, bf16[3,512,512]{2,1,0:T(8,128)(2,1)S(1)} %copy-done.8), kind=kOutput, calls=%fused_computation.16 | convolution fusion | flops 1080032768 | bytes 13117440 | tf_op jit(solution)/shard_map/dot_general | solution.py:83
  106.5 39.7 %psum.22 = f32[512]{0:T(512)} all-reduce(f32[512]{0:T(512)S(1)} %fusion.6), channel_id=1, replica_groups=mesh['row'=4,'grp'=8] {'row','grp'}, use_global_device_ids=true, to_apply=%region_7.8 | all-reduce | flops 512 | bytes 4096 | tf_op jit(solution)/shard_map/psum | solution.py:135
  146.2 91.8 %all-reduce.8.cloned.1.call-done = (f32[3,512,512]{2,1,0:T(8,128)}, f32[512,128]{1,0:T(8,128)}) async-done(((f32[3,512,512]{2,1,0:T(8,128)}, f32[512,128]{1,0:T(8,128)}), (f32[3,512,512]{2,1,0:T(8,128)}, f32[512,128]{1,0:T(8,128)})) %all-reduce.8.cloned.1.call-update) | async-done | bytes 3407888 | tf_op jit(solution)/shard_map/psum | solution.py:135
  238.0 3.9 %copy.51 = f32[3,512,512]{2,1,0:T(8,128)} copy(f32[3,512,512]{2,1,0:T(8,128)} %get-tuple-element.19) | data formatting | bytes 6291456
  241.9 0.0 copy-done.9
  241.9 0.7 copy.52
  (12 shorter events, 0.0 us)
Async XLA Ops:
  7.2 46.8 %copy-start = (bf16[512,128]{1,0:T(8,128)(2,1)S(1)}, bf16[512,128]{1,0:T(8,128)(2,1)}, u32[]{:S(2)}) copy-start(bf16[512,128]{1,0:T(8,128)(2,1)} %param.9) | copy-start | bytes 393220
  7.2 3.5 %copy-start.10 = (f32[512]{0:T(512)S(1)}, f32[512]{0:T(512)}, u32[]{:S(2)}) copy-start(f32[512]{0:T(512)} %param.8) | copy-start | bytes 6148
  7.2 230.8 %all-reduce.8.cloned.1.call-start = ((), (), s32[]{:S(2)}) async-start(), calls=%async_computation | async-start | bytes 6815744 | tf_op jit(solution)/shard_map/psum | solution.py:135
  11.4 5.3 %copy-start.5 = (bf16[16,128,512]{1,2,0:T(8,128)(2,1)}, bf16[16,128,512]{1,2,0:T(8,128)(2,1)S(1)}, u32[]{:S(2)}) copy-start(bf16[16,128,512]{1,2,0:T(8,128)(2,1)S(1)} %fusion.5) | copy-start | bytes 6291460
  24.6 5.0 %copy-start.4 = (bf16[1,16,128,512]{3,2,1,0:T(8,128)(2,1)S(1)}, bf16[1,16,128,512]{3,2,1,0:T(8,128)(2,1)}, u32[]{:S(2)}) copy-start(bf16[1,16,128,512]{3,2,1,0:T(8,128)(2,1)} %copy.25) | copy-start | bytes 6291460
  50.5 13.4 %copy-start.13 = (u32[32]{0:T(128)S(1)}, u32[32]{0:T(128)}, u32[]{:S(2)}) copy-start(u32[32]{0:T(128)} %constant.64) | copy-start | bytes 388
  50.5 14.7 %copy-start.11 = (s32[1,16]{1,0:T(1,128)S(1)}, s32[1,16]{1,0:T(1,128)}, u32[]{:S(2)}) copy-start(s32[1,16]{1,0:T(1,128)} %param.10) | copy-start | bytes 196
  50.5 32.0 %copy-start.12 = (s32[1,16]{1,0:T(1,128)S(1)}, s32[1,16]{1,0:T(1,128)}, u32[]{:S(2)}) copy-start(s32[1,16]{1,0:T(1,128)} %param.11) | copy-start | bytes 196
  82.1 7.7 %copy-start.1 = (f32[2048,512]{1,0:T(8,128)S(1)}, f32[2048,512]{1,0:T(8,128)}, u32[]{:S(2)}) copy-start(f32[2048,512]{1,0:T(8,128)} %add_add_fusion) | copy-start | bytes 12582916
  89.8 2.7 %copy-start.6 = (bf16[16,128,512]{1,2,0:T(8,128)(2,1)S(1)}, bf16[16,128,512]{1,2,0:T(8,128)(2,1)}, u32[]{:S(2)}) copy-start(bf16[16,128,512]{1,2,0:T(8,128)(2,1)} %copy-done.5) | copy-start | bytes 6291460
  92.5 3.7 %copy-start.2 = (bf16[2048,512]{1,0:T(8,128)(2,1)}, bf16[2048,512]{1,0:T(8,128)(2,1)S(1)}, u32[]{:S(2)}) copy-start(bf16[2048,512]{1,0:T(8,128)(2,1)S(1)} %fusion.24) | copy-start | bytes 6291460
  93.9 2.4 copy-start.7
  99.5 3.1 %copy-start.3 = (bf16[2048,512]{1,0:T(8,128)(2,1)S(1)}, bf16[2048,512]{1,0:T(8,128)(2,1)}, u32[]{:S(2)}) copy-start(bf16[2048,512]{1,0:T(8,128)(2,1)} %copy-done.2) | copy-start | bytes 6291460
  99.5 3.1 %copy-start.8 = (bf16[3,512,512]{2,1,0:T(8,128)(2,1)S(1)}, bf16[3,512,512]{2,1,0:T(8,128)(2,1)}, u32[]{:S(2)}) copy-start(bf16[3,512,512]{2,1,0:T(8,128)(2,1)} %param.7) | copy-start | bytes 4718596
  237.9 3.9 %copy-start.9 = (f32[512,128]{1,0:T(8,128)S(1)}, f32[512,128]{1,0:T(8,128)}, u32[]{:S(2)}) copy-start(f32[512,128]{1,0:T(8,128)} %get-tuple-element.21) | copy-start | bytes 786436
Sparse Core Ops, SparseCore 0:
  99.6 138.3 all-reduce.7
where the time goes:
time: 250 us; the launch traced here: 249 us
  waiting for transfers between devices  91.8 us (37%)
  blocking collectives  65.8 us (26%)
  matrix products  30 us (12%)
  local copies, waits for them, and re-layouts  28.7 us (11%)
  other arithmetic  18.1 us (7%)
  between operations  14.9 us (6%)
    psum x1, waiting for transfers between devices, body(): grads = lax.psum((grads[0], grads[1], grads[2]), ('row', 'grp'))  91.8 us
    psum x1, blocking collectives, body(): grads = lax.psum((grads[0], grads[1], grads[2]), ('row', 'grp'))  39.7 us
    dot_general x3, matrix products, encode(): jnp.dot(shifted_input, conv_weight[filter_tap_index], preferred_element_t...  16.7 us
    unnamed x2, blocking collectives  16.4 us
    slice x3, local copies, waits for them, and re-layouts, filter_tap_window(): padded[:, filter_tap_index * spacing:filter_tap_index * spacing + sequenc...  11 us
    all_gather x1, blocking collectives, body(): lax.all_gather(encounter_latent_vector, 'row', axis=0, tiled=True)  9.62 us
    convert_element_type x2, other arithmetic, backward(): jax.vjp(partial(jax.nn.gelu, approximate=True), conv)[1](hidden_grad)[0]  9.38 us
    unnamed x36, local copies, waits for them, and re-layouts  8.5 us
  transfers between devices with their start and end apart: 1, of which 1 were waited for; matrix products, arithmetic and copies ran while one was open for 3% of the time, Pallas kernels for 0%

commit v1 on v0

v1 whole, which is shorter than its diff:
```python
import functools
import math

import jax
import jax.numpy as jnp
from jax import lax
from jax.experimental import pallas as pl
from jax.experimental.pallas import tpu as pltpu
from jax.sharding import PartitionSpec as P

DILATION_GAP = 2
LOGIT_DIVISOR = 0.1
EPS = 1e-05
GELU_A = math.sqrt(2.0 / math.pi)
GELU_B = 0.044715
HIGHEST = lax.Precision.HIGHEST
MESH = pl.DeviceIdType.MESH
F32 = jnp.float32
BF16 = jnp.bfloat16
BLOCK_SEGS = 4


class Links:
    def __init__(self, send_sem, recv_sem):
        self.send_sem, self.recv_sem, self.count, self.copies = send_sem, recv_sem, 0, []

    def send(self, src, dst, device):
        copy = pltpu.make_async_remote_copy(
            src_ref=src,
            dst_ref=dst,
            send_sem=self.send_sem.at[self.count],
            recv_sem=self.recv_sem.at[self.count],
            device_id=device,
            device_id_type=MESH,
        )
        copy.start()
        self.count += 1
        self.copies.append(copy)
        return copy


def shift_rows(values, by, length):
    rows = values.shape[0]
    time = lax.rem(lax.broadcasted_iota(jnp.int32, values.shape, 0), length)
    keep = (time >= by) if by > 0 else (time < length + by)
    return jnp.where(keep, pltpu.roll(values, by % rows, 0), 0.0)


def kernel(
    dims,
    seg_ref,
    w_ref,
    gain_ref,
    head_ref,
    hot_ref,
    pos_ref,
    taps_out,
    proj_out,
    gain_out,
    x3,
    conv,
    n_t,
    unit,
    dgelu,
    pooled,
    hgrad,
    g3,
    embeds,
    acc,
    work,
    r_a1,
    r_b1,
    r_a2,
    r_b2,
    r_z,
    pacc,
    pwork,
    pr_a1,
    pr_b1,
    pr_a2,
    pr_b2,
    pr_z,
    gc,
    gl,
    gh,
    gz,
    send_sem,
    recv_sem,
):
    n_row, n_grp, n_hi, n_lo, n_z, total_segments = dims
    segs, length, chans = seg_ref.shape
    proj = head_ref.shape[1]
    n_taps = w_ref.shape[0]
    half = chans // 2
    quarter = chans // 4
    row = lax.axis_index("row")
    grp = lax.axis_index("grp")
    hi, lo = lax.div(row, n_lo), lax.rem(row, n_lo)
    z, core = lax.div(grp, 2), lax.rem(grp, 2)
    links = Links(send_sem, recv_sem)

    sibling = (row, z * 2 + (1 - core))
    row_peers = [(lax.rem(row + j, n_row), grp) for j in range(1, n_row)]
    lo_peers = [(lax.rem(lo + j, n_lo)) for j in range(1, n_lo)]
    hi_peers = [(lax.rem(hi + j, n_hi)) for j in range(1, n_hi)]
    z_peers = [(lax.rem(z + j, n_z)) for j in range(1, n_z)]

    def lo_dev(p):
        return (hi * n_lo + p, grp)

    def hi_dev(p):
        return (p * n_lo + lo, grp)

    def z_dev(p):
        return (row, p * 2 + core)

    barrier = pltpu.get_barrier_semaphore()
    everyone = [sibling] + row_peers + [z_dev(p) for p in z_peers]
    for device in everyone:
        pl.semaphore_signal(barrier, inc=1, device_id=device, device_id_type=MESH)

    block = BLOCK_SEGS * length

    @pl.loop(0, segs // BLOCK_SEGS)
    def _(b):
        @pl.loop(0, BLOCK_SEGS)
        def _(i):
            s = b * BLOCK_SEGS + i
            inputs = seg_ref[s].astype(F32)
            scale = lax.rsqrt(jnp.mean(inputs * inputs, axis=-1, keepdims=True) + EPS)
            normal = inputs * scale
            unit[s] = normal
            normed = normal * gain_ref[...]
            rows = pl.ds(pl.multiple_of(i * length, length), length)
            x3[rows, 0:chans] = shift_rows(normed, DILATION_GAP, length).astype(BF16)
            x3[rows, chans : 2 * chans] = normed.astype(BF16)
            x3[rows, 2 * chans : 3 * chans] = shift_rows(normed, -DILATION_GAP, length).astype(BF16)
            n_t[s] = normed.T.astype(BF16)

        conv[...] = jnp.dot(
            x3[...], w_ref[...].reshape(n_taps * chans, chans), preferred_element_type=F32
        )

        @pl.loop(0, BLOCK_SEGS)
        def _(i):
            s = b * BLOCK_SEGS + i
            total = jnp.zeros((8, chans), F32)
            step = 32
            for q in range(length // step):
                rows = pl.ds(pl.multiple_of(i * length + q * step, step), step)
                v = conv[rows, :]
                v2 = v * v
                th = jnp.tanh(GELU_A * (v + GELU_B * (v2 * v)))
                cdf = 0.5 * (1.0 + th)
                hidden = seg_ref[s, q * step : (q + 1) * step].astype(F32) + v * cdf
                dgelu[s, q * step : (q + 1) * step] = cdf + (0.5 * GELU_A) * v * (
                    1.0 - th * th
                ) * (1.0 + (3.0 * GELU_B) * v2)
                total = total + hidden.reshape(step // 8, 8, chans).sum(axis=0)
            pooled[pl.ds(s, 1), :] = jnp.sum(total, axis=0, keepdims=True) * (1.0 / length)

    pool16 = pooled[...].astype(BF16)
    projected = jnp.dot(pool16, head_ref[...], preferred_element_type=F32)
    inv = lax.rsqrt(jnp.mean(projected * projected, axis=-1, keepdims=True) + EPS)
    embed = projected * inv * proj ** (-0.5)
    embeds[row, :, 0:proj] = embed
    embeds[row, :, proj:] = hot_ref[...]
    pl.semaphore_wait(barrier, len(everyone))
    moves = [links.send(embeds.at[row], embeds.at[row], device) for device in row_peers]
    for move in moves:
        move.wait_recv()
    every = embeds[...].reshape(n_row * segs, 2 * proj)
    e_all, hot_all = every[:, :proj], every[:, proj:]
    count = n_row * segs
    contract = (((1,), (1,)), ((), ()))

    def scores_of(left):
        return (
            lax.dot_general(left, e_all, contract, precision=HIGHEST, preferred_element_type=F32)
            / LOGIT_DIVISOR
        )

    def same_of(left, first):
        match = lax.dot_general(left, hot_all, contract, preferred_element_type=F32)
        shape = match.shape
        own = first + lax.broadcasted_iota(jnp.int32, shape, 0)
        return jnp.where(own != lax.broadcasted_iota(jnp.int32, shape, 1), match, 0.0)

    s_full, m_full = scores_of(e_all), same_of(hot_all, 0)
    log_row = jnp.log(
        jnp.sum(jnp.where(m_full > 0.5, jnp.exp(s_full), 0.0), axis=0, keepdims=True)
    )
    s_own, m_own = scores_of(embed), same_of(hot_ref[...], row * segs) > 0.5
    log_own = jnp.log(jnp.sum(jnp.where(m_own, jnp.exp(s_own), 0.0), axis=1, keepdims=True))
    mix = jnp.where(m_own, jnp.exp(s_own - log_own) + jnp.exp(s_own - log_row), 0.0)
    mix = mix - jnp.where(
        pos_ref[...] == lax.broadcasted_iota(jnp.int32, (segs, count), 1), 2.0, 0.0
    )
    embed_grad = (total_segments ** (-0.5) / LOGIT_DIVISOR) * jnp.dot(
        mix, e_all, precision=HIGHEST, preferred_element_type=F32
    )
    inner = jnp.mean(embed_grad * projected, axis=-1, keepdims=True)
    projected_grad = proj ** (-0.5) * (embed_grad * inv - projected * (inv * inv * inv * inner))
    hgrad[...] = (
        lax.dot_general(
            projected_grad,
            head_ref[...].astype(F32),
            contract,
            precision=HIGHEST,
            preferred_element_type=F32,
        )
        / length
    )

    @pl.loop(0, segs)
    def _(s):
        grad = (dgelu[s] * hgrad[pl.ds(s, 1), :]).astype(BF16)
        grad32 = grad.astype(F32)
        rows = pl.ds(pl.multiple_of(s * length, length), length)
        shifted = (
            shift_rows(grad32, -DILATION_GAP, length).astype(BF16),
            grad,
            shift_rows(grad32, DILATION_GAP, length).astype(BF16),
        )
        for k in range(n_taps):
            g3[k, 0, rows, :] = shifted[k][:, :half]
            g3[k, 1, rows, :] = shifted[k][:, half:]

    def tiles(values, like):
        need = math.prod(like[:-1])
        if need > values.shape[0]:
            pad = jnp.zeros((need - values.shape[0], values.shape[1]), F32)
            values = jnp.concatenate([values, pad], axis=0)
        return values.reshape(like)

    def own_half(part):
        return pl.ds(pl.multiple_of(core * half, half), half) if part is None else pl.ds(
            pl.multiple_of(core * half + part * quarter, quarter), quarter
        )

    a_cols, b_cols = pl.ds(0, quarter), pl.ds(quarter, quarter)
    every_ = slice(None)

    class Chunk:
        def __init__(self, fill, acc_, work_, ra1, rb1, ra2, rb2, rz, out):
            self.fill, self.acc, self.w, self.out = fill, acc_, work_, out
            self.ra1, self.rb1, self.ra2, self.rb2, self.rz = ra1, rb1, ra2, rb2, rz
            self.moves = []

        def arrive(self):
            for move in self.moves:
                move.wait_recv()
            self.moves = []

        def go(self, src, dst, device):
            self.moves.append(links.send(src, dst, device))

        def stage0(self):
            self.fill(self.acc, 1 - core)
            self.go(self.acc.at[1 - core], self.w, sibling)
            self.fill(self.acc, core)

        def stage1(self):
            self.arrive()
            w = self.w
            w[...] = w[...] + self.acc[core]
            for j, p in enumerate(lo_peers):
                self.go(w.at[:, p, :, :, :, a_cols], self.ra1.at[j], lo_dev(p))
            for j, p in enumerate(hi_peers):
                self.go(w.at[p, :, :, :, :, b_cols], self.rb1.at[j], hi_dev(p))

        def stage2(self):
            self.arrive()
            w = self.w
            a = w[:, lo, :, :, :, a_cols]
            for j in range(n_lo - 1):
                a = a + self.ra1[j]
            w[:, lo, :, :, :, a_cols] = a
            b = w[hi, :, :, :, :, b_cols]
            for j in range(n_hi - 1):
                b = b + self.rb1[j]
            w[hi, :, :, :, :, b_cols] = b
            for j, p in enumerate(hi_peers):
                self.go(w.at[p, lo, :, :, :, a_cols], self.ra2.at[j], hi_dev(p))
            for j, p in enumerate(lo_peers):
                self.go(w.at[hi, p, :, :, :, b_cols], self.rb2.at[j], lo_dev(p))

        def stage3(self):
            self.arrive()
            w = self.w
            a = w[hi, lo, :, :, :, a_cols]
            for j in range(n_hi - 1):
                a = a + self.ra2[j]
            w[hi, lo, :, :, :, a_cols] = a
            b = w[hi, lo, :, :, :, b_cols]
            for j in range(n_lo - 1):
                b = b + self.rb2[j]
            w[hi, lo, :, :, :, b_cols] = b
            for j, p in enumerate(z_peers):
                self.go(w.at[hi, lo, p], self.rz.at[j], z_dev(p))

        def stage4(self):
            self.arrive()
            total = self.w[hi, lo, z]
            for j in range(n_z - 1):
                total = total + self.rz[j]
            place = self.out.at[hi, lo, z, :, :, own_half(None)]
            place[...] = total
            for p in z_peers:
                self.go(place, place, z_dev(p))

        def stage5(self):
            self.arrive()
            place = self.out.at[hi, lo, :, :, :, own_half(0)]
            for p in hi_peers:
                self.go(place, place, hi_dev(p))
            place = self.out.at[hi, lo, :, :, :, own_half(1)]
            for p in lo_peers:
                self.go(place, place, lo_dev(p))

        def stage6(self):
            self.arrive()
            place = self.out.at[:, lo, :, :, :, own_half(0)]
            for p in lo_peers:
                self.go(place, place, lo_dev(p))
            place = self.out.at[hi, :, :, :, :, own_half(1)]
            for p in hi_peers:
                self.go(place, place, hi_dev(p))

        def stage7(self):
            self.arrive()
            place = self.out.at[:, :, :, :, :, own_half(None)]
            self.go(place, place, sibling)

        def stage8(self):
            self.arrive()

    def fill_tap(k, acc_, side):
        total = None
        lhs = jnp.concatenate([n_t[s] for s in range(segs)], axis=1)
        total = jnp.dot(lhs, g3[k, side], preferred_element_type=F32)
        acc_[side] = tiles(total, acc_.shape[1:])

    pool32 = pool16.astype(F32)
    proj_t = lax.dot_general(
        projected_grad,
        pool32,
        (((0,), (0,)), ((), ())),
        precision=HIGHEST,
        preferred_element_type=F32,
    )
    proj_sides = tiles(proj_t[:, :half], pacc.shape[1:]), tiles(proj_t[:, half:], pacc.shape[1:])
    pacc[0] = proj_sides[0]
    pacc[1] = proj_sides[1]

    chunks = [
        Chunk(
            functools.partial(fill_tap, k),
            acc.at[k],
            work.at[k],
            r_a1.at[k],
            r_b1.at[k],
            r_a2.at[k],
            r_b2.at[k],
            r_z.at[k],
            taps_out.at[k],
        )
        for k in range(n_taps)
    ]
    chunks.append(
        Chunk(lambda acc_, side: None, pacc, pwork, pr_a1, pr_b1, pr_a2, pr_b2, pr_z, proj_out)
    )

    gain_state = {"sum": jnp.zeros((8, chans), F32), "moves": []}
    n_pieces = segs // BLOCK_SEGS

    def gain_piece(p):
        rows = slice(p * block, (p + 1) * block)
        lhs = jnp.concatenate(
            [g3[k, side, rows, :] for k in range(n_taps) for side in range(2)], axis=1
        )
        rhs = jnp.concatenate([w_ref[k] for k in range(n_taps)], axis=1)
        back = lax.dot_general(lhs, rhs, contract, preferred_element_type=F32)
        term = back * unit[p * BLOCK_SEGS : (p + 1) * BLOCK_SEGS].reshape(block, chans)
        gain_state["sum"] = gain_state["sum"] + term.reshape(block // 8, 8, chans).sum(axis=0)

    def gain_hop(buffer, index, devices):
        for move in gain_state["moves"]:
            move.wait_recv()
        buffer[index] = gain_state["sum"]
        gain_state["moves"] = [
            links.send(buffer.at[index], buffer.at[index], device) for device in devices
        ]
        gain_state["buffer"] = buffer

    def gain_sum():
        for move in gain_state["moves"]:
            move.wait_recv()
        gain_state["moves"] = []
        buffer = gain_state["buffer"]
        total = buffer[0]
        for j in range(1, buffer.shape[0]):
            total = total + buffer[j]
        gain_state["sum"] = total

    def gain_first():
        gain_state["sum"] = jnp.broadcast_to(
            jnp.sum(gain_state["sum"], axis=0, keepdims=True), (8, chans)
        )
        gain_hop(gc, core, [sibling])

    def gain_lo():
        gain_sum()
        gain_hop(gl, lo, [lo_dev(p) for p in lo_peers])

    def gain_hi():
        gain_sum()
        gain_hop(gh, hi, [hi_dev(p) for p in hi_peers])

    def gain_z():
        gain_sum()
        gain_hop(gz, z, [z_dev(p) for p in z_peers])

    def gain_end():
        gain_sum()
        gain_out[...] = gain_state["sum"]

    extras = [functools.partial(gain_piece, p) for p in range(n_pieces)]
    extras += [gain_first, gain_lo, gain_hi, gain_z, gain_end]

    n_stages = 9
    for step in range(n_stages + len(chunks) - 1):
        for c, chunk in enumerate(chunks):
            stage = step - c
            if 0 <= stage < n_stages:
                getattr(chunk, "stage" + str(stage))()
        if step >= 2 and extras:
            extras.pop(0)()
    while extras:
        extras.pop(0)()
    for copy in links.copies:
        copy.wait_send()


def body(mesh_sizes, segments, conv_weight, gain, head, group, positive):
    n_row, n_grp = mesh_sizes
    n_lo = 2
    n_hi, n_z = n_row // n_lo, n_grp // 2
    shards = n_hi * n_lo * n_z
    records = segments[0]
    segs, length, chans = records.shape
    n_taps = conv_weight.shape[0]
    proj = head.shape[1]
    half, quarter = chans // 2, chans // 4
    count = n_row * segs
    hot = (group[0][:, None] == jnp.arange(proj, dtype=jnp.int32)[None, :]).astype(F32)
    pos = jnp.broadcast_to(positive[0][:, None], (segs, count))
    t = -(-chans // (8 * shards))
    tp = -(-proj // (8 * shards))

    def chunk_shapes(t, lead):
        grid = (n_hi, n_lo, n_z, t, 8)
        return [
            pltpu.VMEM(lead + (2,) + grid + (half,), F32),
            pltpu.VMEM(lead + grid + (half,), F32),
            pltpu.VMEM(lead + (n_lo - 1, n_hi, n_z, t, 8, quarter), F32),
            pltpu.VMEM(lead + (n_hi - 1, n_lo, n_z, t, 8, quarter), F32),
            pltpu.VMEM(lead + (n_hi - 1, n_z, t, 8, quarter), F32),
            pltpu.VMEM(lead + (n_lo - 1, n_z, t, 8, quarter), F32),
            pltpu.VMEM(lead + (n_z - 1, t, 8, half), F32),
        ]

    peers = (n_lo - 1) + (n_hi - 1)
    copies = (n_taps + 1) * 2 * (1 + 2 * peers + n_z - 1)
    copies += (n_row - 1) + 1 + peers + n_z - 1
    rows = segs * length
    scratch = [
        pltpu.VMEM((BLOCK_SEGS * length, n_taps * chans), BF16),
        pltpu.VMEM((BLOCK_SEGS * length, chans), F32),
        pltpu.VMEM((segs, chans, length), BF16),
        pltpu.VMEM((segs, length, chans), F32),
        pltpu.VMEM((segs, length, chans), F32),
        pltpu.VMEM((segs, chans), F32),
        pltpu.VMEM((segs, chans), F32),
        pltpu.VMEM((n_taps, 2, rows, half), BF16),
        pltpu.VMEM((n_row, segs, 2 * proj), F32),
        *chunk_shapes(t, (n_taps,)),
        *chunk_shapes(tp, ()),
        pltpu.VMEM((2, 8, chans), F32),
        pltpu.VMEM((n_lo, 8, chans), F32),
        pltpu.VMEM((n_hi, 8, chans), F32),
        pltpu.VMEM((n_z, 8, chans), F32),
        pltpu.SemaphoreType.DMA((copies,)),
        pltpu.SemaphoreType.DMA((copies,)),
    ]
    vmem = pl.BlockSpec(memory_space=pltpu.VMEM)
    flops = 3 * 2 * rows * chans * chans * n_taps
    taps, projector, gains = pl.pallas_call(
        functools.partial(kernel, (n_row, n_grp, n_hi, n_lo, n_z, count * n_grp)),
        out_shape=(
            jax.ShapeDtypeStruct((n_taps, n_hi, n_lo, n_z, t, 8, chans), F32),
            jax.ShapeDtypeStruct((n_hi, n_lo, n_z, tp, 8, chans), F32),
            jax.ShapeDtypeStruct((8, chans), F32),
        ),
        in_specs=[vmem] * 6,
        out_specs=(vmem,) * 3,
        scratch_shapes=scratch,
        compiler_params=pltpu.CompilerParams(
            collective_id=0, has_side_effects=True, vmem_limit_bytes=60 * 1024 * 1024
        ),
        cost_estimate=pl.CostEstimate(
            flops=flops, bytes_accessed=8 * 1024 * 1024, transcendentals=rows * chans
        ),
    )(records, conv_weight, gain[None, :], head, hot, pos)
    grad_conv = taps.reshape(n_taps, shards * t * 8, chans)[:, :chans]
    projector = projector.reshape(shards * tp * 8, chans)[:proj].T
    return grad_conv, gains[0], projector


def solution(mesh):
    placed = (P("grp", "row", None, None), P(), P(), P(), P("grp", "row"), P("grp", "row"))
    return jax.shard_map(
        functools.partial(body, (mesh.shape["row"], mesh.shape["grp"])),
        mesh=mesh,
        in_specs=placed,
        out_specs=(P(), P(), P()),
        check_vma=False,
    )
```

time: 250 us -> 81.7 us (0.33)
  waiting for transfers between devices: 91.8 us -> 0 us
  Pallas kernels: 0 us -> 71.2 us
  blocking collectives: 65.8 us -> 0 us
  matrix products: 30 us -> 0 us
  local copies, waits for them, and re-layouts: 28.7 us -> 8.26 us
  other arithmetic: 18.1 us -> 1.33 us
  between operations: 14.9 us -> 0.64 us
    psum x1 -> x0, waiting for transfers between devices: 91.8 us -> none  [body(): grads = lax.psum((grads[0], grads[1], grads[2]), ('row', 'grp'))]
    pallas_call x0 -> x1, Pallas kernels: none -> 71.2 us  [body(): pl.pallas_call(functools.partial(kernel, (n_row, n_grp, n_hi, n_lo, n_z,...]
    psum x1 -> x0, blocking collectives: 39.7 us -> none  [body(): grads = lax.psum((grads[0], grads[1], grads[2]), ('row', 'grp'))]
    dot_general x16 -> x0, matrix products: 30 us -> none  [the longest x3 16.7 us: encode(): jnp.dot(shifted_input, conv_weight[filter_tap_index], preferred_element_t...]
    unnamed x2 -> x0, blocking collectives: 16.4 us -> none
    convert_element_type x4 -> x1, other arithmetic: 12.2 us -> 1.33 us  [body(): (group[0][:, None] == jnp.arange(proj, dtype=jnp.int32)[None, :]).astype(...]
    slice x3 -> x1, local copies, waits for them, and re-layouts: 11 us -> 1.3 us  [body(): return (grad_conv, gains[0], projector)]
    all_gather x1 -> x0, blocking collectives: 9.62 us -> none  [body(): lax.all_gather(encounter_latent_vector, 'row', axis=0, tiled=True)]
  transfers between devices with their start and end apart: 1 -> 0, of which waited for: 1 -> 0; matrix products, arithmetic and copies ran while one was open for 3% -> 0% of each run, Pallas kernels for 0% -> 0%
where the time goes in v1:
time: 81.7 us; the launch traced here: 81.4 us
  Pallas kernels  71.2 us (87%)
  local copies, waits for them, and re-layouts  8.26 us (10%)
  other arithmetic  1.33 us (2%)
    pallas_call x1, Pallas kernels, body(): pl.pallas_call(functools.partial(kernel, (n_row, n_grp, n_hi, n_lo, n_z,...  71.2 us
    unnamed x1, local copies, waits for them, and re-layouts  3.86 us
    reshape x1, local copies, waits for them, and re-layouts, body(): projector = projector.reshape(shards * tp * 8, chans)[:proj].T  1.78 us

profile of v1, /device:TPU:0, one launch (start us, length us, event | category | flops | bytes accessed | tf_op | source)
XLA Modules:
  0.0 81.4 jit_solution(16291422824041568221)
XLA Ops:
  0.6 1.3 %fusion.hot_ref = f32[16,128]{1,0:T(8,128)} fusion(s32[16]{0:T(128)} %bitcast.12), kind=kLoop, calls=%fused_computation.1 | loop fusion | flops 4096 | bytes 8256 | tf_op jit(solution)/shard_map/convert_element_type | solution.py:456
  2.0 1.3 %broadcast_in_dim.13.pos_ref = s32[16,64]{1,0:T(8,128)} broadcast(s32[16]{0:T(128)} %bitcast.13), dimensions={0} | broadcast | bytes 4160 | tf_op jit(solution)/shard_map/broadcast_in_dim | solution.py:457
  3.3 71.2 %shard_map.85 = (f32[3,2,2,4,4,8,512]{6,5,4,3,2,1,0:T(8,128)}, f32[2,2,4,1,8,512]{5,4,3,2,1,0:T(8,128)}, f32[8,512]{1,0:T(8,128)}) custom-call(bf16[16,128,512]{2,1,0:T(8,128)(2,1)} %bitcast.14, bf16[3,512,512]{2,1,0:T(8,128)(2,1)} %w_ref.1, f32[1,512]{1,0:T(1,128)} %bitcast.15, bf16[512,128]{1,0:T(8,128)(2,1)} %head_ref.1, f32[16,128]{1,0:T(8,128)} %fusion.hot_ref, ...), custom_call_target="tpu_custom_call" | custom-call | flops 9663676416 | bytes 8388608 | tf_op jit(solution)/shard_map/pallas_call | solution.py:498
  74.5 1.3 %slice.3 = f32[1,512]{1,0:T(1,128)} slice(f32[8,512]{1,0:T(8,128)} %get-tuple-element.7), slice={[0:1], [0:512]} | slice | bytes 4096 | tf_op jit(solution)/shard_map/slice | solution.py:517
  75.8 1.8 %copy.9 = f32[128,512]{0,1:T(8,128)} copy(f32[128,512]{1,0:T(8,128)} %bitcast.10) | data formatting | bytes 524288 | tf_op jit(solution)/shard_map/reshape | solution.py:516
  77.5 3.9 %copy.11 = f32[3,512,512]{2,1,0:T(8,128)} copy(f32[3,512,512]{2,1,0:T(8,128)} %bitcast.8) | data formatting | bytes 6291456

commit v2 on v1

v2 whole, which is shorter than its diff:
```python
import functools
import math

import jax
import jax.numpy as jnp
from jax import lax
from jax.experimental import pallas as pl
from jax.experimental.pallas import tpu as pltpu
from jax.sharding import PartitionSpec as P

DILATION_GAP = 2
LOGIT_DIVISOR = 0.1
EPS = 1e-05
GELU_A = math.sqrt(2.0 / math.pi)
GELU_B = 0.044715
HIGHEST = lax.Precision.HIGHEST
MESH = pl.DeviceIdType.MESH
F32 = jnp.float32
BF16 = jnp.bfloat16
BLOCK_SEGS = 4
PARTS = 2


class Links:
    def __init__(self, send_sem, recv_sem):
        self.send_sem, self.recv_sem, self.count, self.copies = send_sem, recv_sem, 0, []

    def send(self, src, dst, device):
        copy = pltpu.make_async_remote_copy(
            src_ref=src,
            dst_ref=dst,
            send_sem=self.send_sem.at[self.count],
            recv_sem=self.recv_sem.at[self.count],
            device_id=device,
            device_id_type=MESH,
        )
        copy.start()
        self.count += 1
        self.copies.append(copy)
        return copy


def shift_rows(values, by, length):
    moved = pltpu.roll(values, by % length, 0)
    edge = moved[:8] if by > 0 else moved[length - 8 :]
    time = lax.broadcasted_iota(jnp.int32, edge.shape, 0)
    edge = jnp.where((time >= by) if by > 0 else (time < 8 + by), edge, 0.0)
    pieces = [edge, moved[8:]] if by > 0 else [moved[: length - 8], edge]
    return jnp.concatenate(pieces, axis=0)


def as_column(line):
    n = line.shape[1]
    square = lax.broadcasted_iota(jnp.int32, (n, n), 0) == lax.broadcasted_iota(
        jnp.int32, (n, n), 1
    )
    return jnp.sum(jnp.where(square, line.astype(F32), 0.0), axis=1, keepdims=True)


def kernel(
    dims,
    seg_hbm,
    w_hbm,
    gain_ref,
    head_ref,
    group_ref,
    pos_ref,
    taps_out,
    proj_out,
    gain_out,
    seg_ref,
    w_ref,
    x3,
    conv,
    n_t,
    unit,
    dgelu,
    pooled,
    hgrad,
    g3,
    embeds,
    acc,
    work,
    r_a1,
    r_b1,
    r_a2,
    r_b2,
    r_z,
    full,
    pacc,
    pwork,
    pr_a1,
    pr_b1,
    pr_a2,
    pr_b2,
    pr_z,
    pfull,
    gc,
    gl,
    gh,
    gz,
    send_sem,
    recv_sem,
    load_sem,
    store_sem,
):
    n_row, n_grp, n_hi, n_lo, n_z, total_segments = dims
    segs, length, chans = seg_ref.shape
    proj = head_ref.shape[1]
    n_taps = w_ref.shape[0]
    half = chans // 2
    quarter = chans // 4
    row = lax.axis_index("row")
    grp = lax.axis_index("grp")
    hi, lo = lax.div(row, n_lo), lax.rem(row, n_lo)
    z, core = lax.div(grp, 2), lax.rem(grp, 2)
    links = Links(send_sem, recv_sem)

    sibling = (row, z * 2 + (1 - core))
    row_peers = [(lax.rem(row + j, n_row), grp) for j in range(1, n_row)]
    lo_peers = [(lax.rem(lo + j, n_lo)) for j in range(1, n_lo)]
    hi_peers = [(lax.rem(hi + j, n_hi)) for j in range(1, n_hi)]
    z_peers = [(lax.rem(z + j, n_z)) for j in range(1, n_z)]

    def lo_dev(p):
        return (hi * n_lo + p, grp)

    def hi_dev(p):
        return (p * n_lo + lo, grp)

    def z_dev(p):
        return (row, p * 2 + core)

    barrier = pltpu.get_barrier_semaphore()
    everyone = [sibling] + row_peers + [z_dev(p) for p in z_peers]
    for device in everyone:
        pl.semaphore_signal(barrier, inc=1, device_id=device, device_id_type=MESH)

    block = BLOCK_SEGS * length
    n_blocks = segs // BLOCK_SEGS

    def seg_load(b):
        part = pl.ds(b * BLOCK_SEGS, BLOCK_SEGS)
        return pltpu.make_async_copy(seg_hbm.at[part], seg_ref.at[part], load_sem.at[b])

    w_load = pltpu.make_async_copy(w_hbm, w_ref, load_sem.at[n_blocks])
    seg_load(0).start()
    w_load.start()
    for b in range(1, n_blocks):
        seg_load(b).start()
    group_one = as_column(group_ref[...]).astype(jnp.int32)
    hot = jnp.where(
        group_one == lax.broadcasted_iota(jnp.int32, (segs, proj), 1), 1.0, 0.0
    ).astype(F32)
    embeds[row, :, proj:] = hot
    w_load.wait()

    @pl.loop(0, n_blocks)
    def _(b):
        seg_load(b).wait()

        @pl.loop(0, BLOCK_SEGS)
        def _(i):
            s = b * BLOCK_SEGS + i
            inputs = seg_ref[s].astype(F32)
            scale = lax.rsqrt(jnp.mean(inputs * inputs, axis=-1, keepdims=True) + EPS)
            normal = inputs * scale
            unit[s] = normal
            normed = normal * gain_ref[...]
            rows = pl.ds(pl.multiple_of(i * length, length), length)
            x3[rows, 0:chans] = shift_rows(normed, DILATION_GAP, length).astype(BF16)
            x3[rows, chans : 2 * chans] = normed.astype(BF16)
            x3[rows, 2 * chans : 3 * chans] = shift_rows(normed, -DILATION_GAP, length).astype(BF16)
            n_t[s] = normed.T.astype(BF16)

        conv[...] = jnp.dot(
            x3[...], w_ref[...].reshape(n_taps * chans, chans), preferred_element_type=F32
        )

        @pl.loop(0, BLOCK_SEGS)
        def _(i):
            s = b * BLOCK_SEGS + i
            total = jnp.zeros((8, chans), F32)
            step = 32
            for q in range(length // step):
                rows = pl.ds(pl.multiple_of(i * length + q * step, step), step)
                v = conv[rows, :]
                v2 = v * v
                th = jnp.tanh(GELU_A * (v + GELU_B * (v2 * v)))
                cdf = 0.5 * (1.0 + th)
                hidden = seg_ref[s, q * step : (q + 1) * step].astype(F32) + v * cdf
                dgelu[s, q * step : (q + 1) * step] = cdf + (0.5 * GELU_A) * v * (
                    1.0 - th * th
                ) * (1.0 + (3.0 * GELU_B) * v2)
                total = total + hidden.reshape(step // 8, 8, chans).sum(axis=0)
            pooled[pl.ds(s, 1), :] = jnp.sum(total, axis=0, keepdims=True) * (1.0 / length)

    pool16 = pooled[...].astype(BF16)
    projected = jnp.dot(pool16, head_ref[...], preferred_element_type=F32)
    inv = lax.rsqrt(jnp.mean(projected * projected, axis=-1, keepdims=True) + EPS)
    embed = projected * inv * proj ** (-0.5)
    embeds[row, :, 0:proj] = embed
    pl.semaphore_wait(barrier, len(everyone))
    moves = [links.send(embeds.at[row], embeds.at[row], device) for device in row_peers]
    for move in moves:
        move.wait_recv()
    every = embeds[...].reshape(n_row * segs, 2 * proj)
    e_all, hot_all = every[:, :proj], every[:, proj:]
    count = n_row * segs
    contract = (((1,), (1,)), ((), ()))

    def scores_of(left):
        return (
            lax.dot_general(left, e_all, contract, precision=HIGHEST, preferred_element_type=F32)
            / LOGIT_DIVISOR
        )

    def same_of(left, first):
        match = lax.dot_general(left, hot_all, contract, preferred_element_type=F32)
        shape = match.shape
        own = first + lax.broadcasted_iota(jnp.int32, shape, 0)
        return jnp.where(own != lax.broadcasted_iota(jnp.int32, shape, 1), match, 0.0)

    s_full, m_full = scores_of(e_all), same_of(hot_all, 0)
    log_row = jnp.log(
        jnp.sum(jnp.where(m_full > 0.5, jnp.exp(s_full), 0.0), axis=0, keepdims=True)
    )
    s_own, m_own = scores_of(embed), same_of(hot, row * segs) > 0.5
    log_own = jnp.log(jnp.sum(jnp.where(m_own, jnp.exp(s_own), 0.0), axis=1, keepdims=True))
    mix = jnp.where(m_own, jnp.exp(s_own - log_own) + jnp.exp(s_own - log_row), 0.0)
    mix = mix - jnp.where(
        as_column(pos_ref[...]).astype(jnp.int32)
        == lax.broadcasted_iota(jnp.int32, (segs, count), 1),
        2.0,
        0.0,
    )
    embed_grad = (total_segments ** (-0.5) / LOGIT_DIVISOR) * jnp.dot(
        mix, e_all, precision=HIGHEST, preferred_element_type=F32
    )
    inner = jnp.mean(embed_grad * projected, axis=-1, keepdims=True)
    projected_grad = proj ** (-0.5) * (embed_grad * inv - projected * (inv * inv * inv * inner))
    hgrad[...] = (
        lax.dot_general(
            projected_grad,
            head_ref[...].astype(F32),
            contract,
            precision=HIGHEST,
            preferred_element_type=F32,
        )
        / length
    )

    def tiles(values, like):
        need = math.prod(like[:-1])
        if need > values.shape[0]:
            pad = jnp.zeros((need - values.shape[0], values.shape[1]), F32)
            values = jnp.concatenate([values, pad], axis=0)
        return values.reshape(like)

    class Chunk:
        def __init__(self, fill, finish, buffers):
            self.fill, self.finish = fill, finish
            self.acc, self.w, self.ra1, self.rb1, self.ra2, self.rb2, self.rz, self.out = buffers
            self.moves = []

        def arrive(self):
            for move in self.moves:
                move.wait_recv()
            self.moves = []

        def go(self, src, dst, device):
            self.moves.append(links.send(src, dst, device))

        def stage0(self):
            self.fill(self.acc, 1 - core)
            self.go(self.acc.at[1 - core], self.w, sibling)
            self.fill(self.acc, core)

        def stage1(self):
            self.arrive()
            w = self.w
            w[...] = w[...] + self.acc[core]
            for j, p in enumerate(lo_peers):
                self.go(w.at[0, :, p], self.ra1.at[j], lo_dev(p))
            for j, p in enumerate(hi_peers):
                self.go(w.at[1, p], self.rb1.at[j], hi_dev(p))

        def stage2(self):
            self.arrive()
            w = self.w
            a = w[0, :, lo]
            for j in range(n_lo - 1):
                a = a + self.ra1[j]
            w[0, :, lo] = a
            b = w[1, hi]
            for j in range(n_hi - 1):
                b = b + self.rb1[j]
            w[1, hi] = b
            for j, p in enumerate(hi_peers):
                self.go(w.at[0, p, lo], self.ra2.at[j], hi_dev(p))
            for j, p in enumerate(lo_peers):
                self.go(w.at[1, hi, p], self.rb2.at[j], lo_dev(p))

        def stage3(self):
            self.arrive()
            w = self.w
            a = w[0, hi, lo]
            for j in range(n_hi - 1):
                a = a + self.ra2[j]
            w[0, hi, lo] = a
            b = w[1, hi, lo]
            for j in range(n_lo - 1):
                b = b + self.rb2[j]
            w[1, hi, lo] = b
            for j, p in enumerate(z_peers):
                self.go(w.at[:, hi, lo, p], self.rz.at[j], z_dev(p))

        def stage4(self):
            self.arrive()
            total = self.w[:, hi, lo, z]
            for j in range(n_z - 1):
                total = total + self.rz[j]
            self.out[core, :, hi, lo, z] = total
            place = self.out.at[core, :, hi, lo, z]
            for p in z_peers:
                self.go(place, place, z_dev(p))

        def stage5(self):
            self.arrive()
            place = self.out.at[core, 0, hi, lo]
            for p in hi_peers:
                self.go(place, place, hi_dev(p))
            place = self.out.at[core, 1, hi, lo]
            for p in lo_peers:
                self.go(place, place, lo_dev(p))

        def stage6(self):
            self.arrive()
            place = self.out.at[core, 0, :, lo]
            for p in lo_peers:
                self.go(place, place, lo_dev(p))
            place = self.out.at[core, 1, hi]
            for p in hi_peers:
                self.go(place, place, hi_dev(p))

        def stage7(self):
            self.arrive()
            place = self.out.at[core]
            self.go(place, place, sibling)

        def stage8(self):
            self.arrive()
            self.finish()

    def put(acc_, side, values):
        for part in range(2):
            acc_[side, part] = tiles(
                values[:, part * quarter : (part + 1) * quarter], acc_.shape[2:]
            )

    parts = acc.shape[0] // n_taps
    part_rows = chans // parts

    def fill_tap(c, acc_, side):
        k, part = c // parts, c % parts
        first = part * part_rows
        lhs = jnp.concatenate([n_t[s, first : first + part_rows] for s in range(segs)], axis=1)
        put(acc_, side, jnp.dot(lhs, g3[k, side], preferred_element_type=F32))

    stores = []

    def store_tap(c):
        for side in range(2):
            for part in range(2):
                first = side * half + part * quarter
                store = pltpu.make_async_copy(
                    full.at[c, side, part],
                    taps_out.at[c, :, :, :, :, :, pl.ds(first, quarter)],
                    store_sem.at[len(stores)],
                )
                store.start()
                stores.append(store)

    def store_proj():
        for side in range(2):
            for part in range(2):
                first = side * half + part * quarter
                block_t = pfull[side, part].reshape(-1, quarter)[:proj]
                proj_out[first : first + quarter, :] = block_t.T

    pool32 = pool16.astype(F32)
    proj_t = lax.dot_general(
        projected_grad,
        pool32,
        (((0,), (0,)), ((), ())),
        precision=HIGHEST,
        preferred_element_type=F32,
    )
    for side in range(2):
        put(pacc, side, proj_t[:, side * half : (side + 1) * half])

    proj_buffers = (pacc, pwork, pr_a1, pr_b1, pr_a2, pr_b2, pr_z, pfull)
    tap_buffers = (acc, work, r_a1, r_b1, r_a2, r_b2, r_z, full)
    chunks = [Chunk(lambda acc_, side: None, store_proj, proj_buffers)]
    chunks += [
        Chunk(
            functools.partial(fill_tap, c),
            functools.partial(store_tap, c),
            [buffer.at[c] for buffer in tap_buffers],
        )
        for c in range(n_taps * parts)
    ]
    chunks[0].stage0()

    @pl.loop(0, segs)
    def _(s):
        grad = (dgelu[s] * hgrad[pl.ds(s, 1), :]).astype(BF16)
        grad32 = grad.astype(F32)
        rows = pl.ds(pl.multiple_of(s * length, length), length)
        shifted = (
            shift_rows(grad32, -DILATION_GAP, length).astype(BF16),
            grad,
            shift_rows(grad32, DILATION_GAP, length).astype(BF16),
        )
        for k in range(n_taps):
            g3[k, 0, rows, :] = shifted[k][:, :half]
            g3[k, 1, rows, :] = shifted[k][:, half:]

    gain_state = {"sum": jnp.zeros((8, chans), F32), "moves": []}
    n_pieces = segs // BLOCK_SEGS

    def gain_piece(p):
        rows = slice(p * block, (p + 1) * block)
        lhs = jnp.concatenate(
            [g3[k, side, rows, :] for k in range(n_taps) for side in range(2)], axis=1
        )
        rhs = jnp.concatenate([w_ref[k] for k in range(n_taps)], axis=1)
        back = lax.dot_general(lhs, rhs, contract, preferred_element_type=F32)
        term = back * unit[p * BLOCK_SEGS : (p + 1) * BLOCK_SEGS].reshape(block, chans)
        gain_state["sum"] = gain_state["sum"] + term.reshape(block // 8, 8, chans).sum(axis=0)

    def gain_hop(buffer, index, devices):
        for move in gain_state["moves"]:
            move.wait_recv()
        buffer[index] = gain_state["sum"]
        gain_state["moves"] = [
            links.send(buffer.at[index], buffer.at[index], device) for device in devices
        ]
        gain_state["buffer"] = buffer

    def gain_sum():
        for move in gain_state["moves"]:
            move.wait_recv()
        gain_state["moves"] = []
        buffer = gain_state["buffer"]
        total = buffer[0]
        for j in range(1, buffer.shape[0]):
            total = total + buffer[j]
        gain_state["sum"] = total

    def gain_first():
        gain_state["sum"] = jnp.broadcast_to(
            jnp.sum(gain_state["sum"], axis=0, keepdims=True), (8, chans)
        )
        gain_hop(gc, core, [sibling])

    def gain_lo():
        gain_sum()
        gain_hop(gl, lo, [lo_dev(p) for p in lo_peers])

    def gain_hi():
        gain_sum()
        gain_hop(gh, hi, [hi_dev(p) for p in hi_peers])

    def gain_z():
        gain_sum()
        gain_hop(gz, z, [z_dev(p) for p in z_peers])

    def gain_end():
        gain_sum()
        gain_out[...] = gain_state["sum"][:1]

    extras = [functools.partial(gain_piece, p) for p in range(n_pieces)]
    extras += [gain_first, gain_lo, gain_hi, gain_z, gain_end]

    n_stages = 9
    for step in range(n_stages + len(chunks) - 1):
        for c, chunk in enumerate(chunks):
            stage = step - c
            if 0 <= stage < n_stages and (step > 0 or c > 0):
                getattr(chunk, "stage" + str(stage))()
        if step >= 2 and extras:
            extras.pop(0)()
    while extras:
        extras.pop(0)()
    for copy in links.copies:
        copy.wait_send()
    for store in stores:
        store.wait()


def place_kernel(taps, projector, gains, taps_out, projector_out, gains_out, sems):
    pairs = [(taps.at[c], taps_out.at[c]) for c in range(taps.shape[0])]
    pairs += [(projector, projector_out), (gains, gains_out)]
    copies = [pltpu.make_async_copy(*pair, sems.at[i]) for i, pair in enumerate(pairs)]
    for copy in copies:
        copy.start()
    for copy in copies:
        copy.wait()


def body(mesh_sizes, segments, conv_weight, gain, head, group, positive):
    n_row, n_grp = mesh_sizes
    n_lo = 2
    n_hi, n_z = n_row // n_lo, n_grp // 2
    shards = n_hi * n_lo * n_z
    records = segments[0]
    segs, length, chans = records.shape
    n_taps = conv_weight.shape[0]
    proj = head.shape[1]
    half, quarter = chans // 2, chans // 4
    count = n_row * segs
    parts = max(1, min(PARTS, chans // (8 * shards)))
    n_chunks = n_taps * parts
    t = -(-chans // (8 * shards * parts))
    tp = -(-proj // (8 * shards))

    def chunk_shapes(t, lead):
        grid = (n_hi, n_lo, n_z, t, 8)
        return [
            pltpu.VMEM(lead + (2, 2) + grid + (quarter,), F32),
            pltpu.VMEM(lead + (2,) + grid + (quarter,), F32),
            pltpu.VMEM(lead + (n_lo - 1, n_hi, n_z, t, 8, quarter), F32),
            pltpu.VMEM(lead + (n_hi - 1, n_lo, n_z, t, 8, quarter), F32),
            pltpu.VMEM(lead + (n_hi - 1, n_z, t, 8, quarter), F32),
            pltpu.VMEM(lead + (n_lo - 1, n_z, t, 8, quarter), F32),
            pltpu.VMEM(lead + (n_z - 1, 2, t, 8, quarter), F32),
            pltpu.VMEM(lead + (2, 2) + grid + (quarter,), F32),
        ]

    peers = (n_lo - 1) + (n_hi - 1)
    copies = (n_chunks + 1) * 2 * (1 + 2 * peers + n_z - 1)
    copies += (n_row - 1) + 1 + peers + n_z - 1
    rows = segs * length
    scratch = [
        pltpu.VMEM(records.shape, BF16),
        pltpu.VMEM(conv_weight.shape, BF16),
        pltpu.VMEM((BLOCK_SEGS * length, n_taps * chans), BF16),
        pltpu.VMEM((BLOCK_SEGS * length, chans), F32),
        pltpu.VMEM((segs, chans, length), BF16),
        pltpu.VMEM((segs, length, chans), F32),
        pltpu.VMEM((segs, length, chans), F32),
        pltpu.VMEM((segs, chans), F32),
        pltpu.VMEM((segs, chans), F32),
        pltpu.VMEM((n_taps, 2, rows, half), BF16),
        pltpu.VMEM((n_row, segs, 2 * proj), F32),
        *chunk_shapes(t, (n_chunks,)),
        *chunk_shapes(tp, ()),
        pltpu.VMEM((2, 8, chans), F32),
        pltpu.VMEM((n_lo, 8, chans), F32),
        pltpu.VMEM((n_hi, 8, chans), F32),
        pltpu.VMEM((n_z, 8, chans), F32),
        pltpu.SemaphoreType.DMA((copies,)),
        pltpu.SemaphoreType.DMA((copies,)),
        pltpu.SemaphoreType.DMA((segs // BLOCK_SEGS + 1,)),
        pltpu.SemaphoreType.DMA((n_chunks * 4,)),
    ]
    vmem = pl.BlockSpec(memory_space=pltpu.VMEM)
    anywhere = pl.BlockSpec(memory_space=pl.ANY)
    flops = 3 * 2 * rows * chans * chans * n_taps
    taps, projector, gains = pl.pallas_call(
        functools.partial(kernel, (n_row, n_grp, n_hi, n_lo, n_z, count * n_grp)),
        out_shape=(
            jax.ShapeDtypeStruct((n_chunks, n_hi, n_lo, n_z, t, 8, chans), F32),
            jax.ShapeDtypeStruct((chans, proj), F32),
            jax.ShapeDtypeStruct((1, chans), F32),
        ),
        in_specs=[anywhere] * 2 + [vmem] * 4,
        out_specs=(anywhere, vmem, vmem),
        scratch_shapes=scratch,
        compiler_params=pltpu.CompilerParams(
            collective_id=0, has_side_effects=True, vmem_limit_bytes=60 * 1024 * 1024
        ),
        cost_estimate=pl.CostEstimate(
            flops=flops, bytes_accessed=8 * 1024 * 1024, transcendentals=rows * chans
        ),
    )(records, conv_weight, gain[None, :], head, group, positive)
    results = (taps, projector, gains)
    taps, projector, gains = pl.pallas_call(
        place_kernel,
        out_shape=tuple(jax.ShapeDtypeStruct(r.shape, F32) for r in results),
        in_specs=[anywhere] * 3,
        out_specs=(anywhere,) * 3,
        scratch_shapes=[pltpu.SemaphoreType.DMA((n_chunks + 2,))],
        compiler_params=pltpu.CompilerParams(vmem_limit_bytes=60 * 1024 * 1024),
    )(*results)
    rows_each = chans // parts
    taps = taps.reshape(n_chunks, shards * t * 8, chans)[:, :rows_each]
    return taps.reshape(n_taps, chans, chans), gains.reshape(chans), projector


def solution(mesh):
    placed = (P("grp", "row", None, None), P(), P(), P(), P("grp", "row"), P("grp", "row"))
    return jax.shard_map(
        functools.partial(body, (mesh.shape["row"], mesh.shape["grp"])),
        mesh=mesh,
        in_specs=placed,
        out_specs=(P(), P(), P()),
        check_vma=False,
    )
```

time: 81.7 us -> 180 us (2.20)
  Pallas kernels: 71.2 us -> 178 us
  local copies, waits for them, and re-layouts: 8.26 us -> 0 us
    pallas_call x0 -> x1, Pallas kernels: none -> 104 us  [body(): pl.pallas_call(place_kernel, out_shape=tuple((jax.ShapeDtypeStruct(r.shap...]
    unnamed x1 -> x0, local copies, waits for them, and re-layouts: 3.86 us -> none
    pallas_call x1, Pallas kernels: 71.2 us -> 74 us  [body(): pl.pallas_call(functools.partial(kernel, (n_row, n_grp, n_hi, n_lo, n_z,...]
where the time goes in v2:
time: 180 us; the launch traced here: 179 us
  Pallas kernels  178 us (99%)
    pallas_call x1, Pallas kernels, body(): pl.pallas_call(place_kernel, out_shape=tuple((jax.ShapeDtypeStruct(r.shap...  104 us
    pallas_call x1, Pallas kernels, body(): pl.pallas_call(functools.partial(kernel, (n_row, n_grp, n_hi, n_lo, n_z,...  74 us

profile of v2, /device:TPU:0, one launch (start us, length us, event | category | flops | bytes accessed | tf_op | source)
XLA Modules:
  0.0 179.1 jit_solution(5295132478105659017)
XLA Ops:
  0.6 74.0 %shard_map.85 = (f32[6,2,2,4,2,8,512]{6,5,4,3,2,1,0:T(8,128)}, f32[512,128]{1,0:T(8,128)}, f32[1,512]{1,0:T(1,128)}) custom-call(bf16[16,128,512]{2,1,0:T(8,128)(2,1)} %bitcast.5, bf16[3,512,512]{2,1,0:T(8,128)(2,1)} %w_hbm.1, f32[1,512]{1,0:T(1,128)} %bitcast.6, bf16[512,128]{1,0:T(8,128)(2,1)} %head_ref.1, s32[1,16]{1,0:T(1,128)} %group_ref.1, s32[1,16]{1,0:T(1,128)} %pos_ref.1), custom_call_target="tpu_custom_call" | custom-call | flops 9663676416 | bytes 8388608 | tf_op jit(solution)/shard_map/pallas_call | solution.py:571
  74.6 104.5 %shard_map.86 = (f32[6,2,2,4,2,8,512]{6,5,4,3,2,1,0:T(8,128)}, f32[512,128]{1,0:T(8,128)}, f32[1,512]{1,0:T(1,128)}) custom-call(f32[6,2,2,4,2,8,512]{6,5,4,3,2,1,0:T(8,128)} %get-tuple-element.9.taps, f32[512,128]{1,0:T(8,128)} %get-tuple-element.10.projector, f32[1,512]{1,0:T(1,128)} %get-tuple-element.11.gains), custom_call_target="tpu_custom_call" | custom-call | tf_op jit(solution)/shard_map/pallas_call | solution.py:589

commit v3 on v2

--- a/solution.py
+++ b/solution.py
@@ -18,7 +18,8 @@
 F32 = jnp.float32
 BF16 = jnp.bfloat16
 BLOCK_SEGS = 4
-PARTS = 2
+PARTS = 1
+PLACE_ROWS = 256
 
 
 class Links:
@@ -408,23 +409,29 @@
             functools.partial(store_tap, c),
             [buffer.at[c] for buffer in tap_buffers],
         )
-        for c in range(n_taps * parts)
+        for c in sorted(range(n_taps * parts), key=lambda c: c // parts != n_taps // 2)
     ]
     chunks[0].stage0()
+
+    middle = n_taps // 2
 
     @pl.loop(0, segs)
     def _(s):
         grad = (dgelu[s] * hgrad[pl.ds(s, 1), :]).astype(BF16)
-        grad32 = grad.astype(F32)
         rows = pl.ds(pl.multiple_of(s * length, length), length)
-        shifted = (
-            shift_rows(grad32, -DILATION_GAP, length).astype(BF16),
-            grad,
-            shift_rows(grad32, DILATION_GAP, length).astype(BF16),
-        )
-        for k in range(n_taps):
-            g3[k, 0, rows, :] = shifted[k][:, :half]
-            g3[k, 1, rows, :] = shifted[k][:, half:]
+        for side in range(2):
+            g3[middle, side, rows, :] = grad[:, side * half : (side + 1) * half]
+
+    def shift_grads():
+        @pl.loop(0, segs)
+        def _(s):
+            rows = pl.ds(pl.multiple_of(s * length, length), length)
+            for side in range(2):
+                grad = g3[middle, side, rows, :].astype(F32)
+                for k in range(n_taps):
+                    if k != middle:
+                        by = (k - middle) * DILATION_GAP
+                        g3[k, side, rows, :] = shift_rows(grad, by, length).astype(BF16)
 
     gain_state = {"sum": jnp.zeros((8, chans), F32), "moves": []}
     n_pieces = segs // BLOCK_SEGS
@@ -489,7 +496,9 @@
             stage = step - c
             if 0 <= stage < n_stages and (step > 0 or c > 0):
                 getattr(chunk, "stage" + str(stage))()
-        if step >= 2 and extras:
+        if step == parts:
+            shift_grads()
+        if step >= 3 and extras:
             extras.pop(0)()
     while extras:
         extras.pop(0)()
@@ -499,14 +508,10 @@
         store.wait()
 
 
-def place_kernel(taps, projector, gains, taps_out, projector_out, gains_out, sems):
-    pairs = [(taps.at[c], taps_out.at[c]) for c in range(taps.shape[0])]
-    pairs += [(projector, projector_out), (gains, gains_out)]
-    copies = [pltpu.make_async_copy(*pair, sems.at[i]) for i, pair in enumerate(pairs)]
-    for copy in copies:
-        copy.start()
-    for copy in copies:
-        copy.wait()
+def place_kernel(taps, projector, gains, taps_out, projector_out, gains_out):
+    taps_out[...] = taps[...]
+    projector_out[...] = projector[...]
+    gains_out[...] = gains[...]
 
 
 def body(mesh_sizes, segments, conv_weight, gain, head, group, positive):
@@ -585,17 +590,26 @@
             flops=flops, bytes_accessed=8 * 1024 * 1024, transcendentals=rows * chans
         ),
     )(records, conv_weight, gain[None, :], head, group, positive)
-    results = (taps, projector, gains)
+    taps = taps.reshape(n_chunks, shards * t * 8, chans)
+    rows_each = chans // parts
+    pieces = rows_each // PLACE_ROWS
+    places = (
+        pl.BlockSpec((1, PLACE_ROWS, chans), lambda i: (i // pieces, i % pieces, 0)),
+        pl.BlockSpec((chans, proj), lambda i: (0, 0)),
+        pl.BlockSpec((1, chans), lambda i: (0, 0)),
+    )
     taps, projector, gains = pl.pallas_call(
         place_kernel,
-        out_shape=tuple(jax.ShapeDtypeStruct(r.shape, F32) for r in results),
-        in_specs=[anywhere] * 3,
-        out_specs=(anywhere,) * 3,
-        scratch_shapes=[pltpu.SemaphoreType.DMA((n_chunks + 2,))],
+        grid=(n_chunks * pieces,),
+        out_shape=(
+            jax.ShapeDtypeStruct((n_chunks, rows_each, chans), F32),
+            jax.ShapeDtypeStruct((chans, proj), F32),
+            jax.ShapeDtypeStruct((1, chans), F32),
+        ),
+        in_specs=places,
+        out_specs=places,
         compiler_params=pltpu.CompilerParams(vmem_limit_bytes=60 * 1024 * 1024),
-    )(*results)
-    rows_each = chans // parts
-    taps = taps.reshape(n_chunks, shards * t * 8, chans)[:, :rows_each]
+    )(taps, projector, gains)
     return taps.reshape(n_taps, chans, chans), gains.reshape(chans), projector
 
 

time: 180 us -> 77.2 us (0.43)
  Pallas kernels: 178 us -> 76.3 us
    pallas_call x1, Pallas kernels: 104 us -> 5.46 us  [body(): pl.pallas_call(place_kernel, grid=(n_chunks * pieces,), out_shape=(jax.Sh...]
    pallas_call x1, Pallas kernels: 74 us -> 70.9 us  [body(): pl.pallas_call(functools.partial(kernel, (n_row, n_grp, n_hi, n_lo, n_z,...]
where the time goes in v3:
time: 77.2 us; the launch traced here: 77 us
  Pallas kernels  76.3 us (99%)
    pallas_call x1, Pallas kernels, body(): pl.pallas_call(functools.partial(kernel, (n_row, n_grp, n_hi, n_lo, n_z,...  70.9 us
    pallas_call x1, Pallas kernels, body(): pl.pallas_call(place_kernel, grid=(n_chunks * pieces,), out_shape=(jax.Sh...  5.46 us

profile of v3, /device:TPU:0, one launch (start us, length us, event | category | flops | bytes accessed | tf_op | source)
XLA Modules:
  0.0 77.0 jit_solution(6084534973832339834)
XLA Ops:
  0.6 70.9 %shard_map.85 = (f32[3,2,2,4,4,8,512]{6,5,4,3,2,1,0:T(8,128)}, f32[512,128]{1,0:T(8,128)}, f32[1,512]{1,0:T(1,128)}) custom-call(bf16[16,128,512]{2,1,0:T(8,128)(2,1)} %bitcast.5, bf16[3,512,512]{2,1,0:T(8,128)(2,1)} %w_hbm.1, f32[1,512]{1,0:T(1,128)} %bitcast.6, bf16[512,128]{1,0:T(8,128)(2,1)} %head_ref.1, s32[1,16]{1,0:T(1,128)} %group_ref.1, s32[1,16]{1,0:T(1,128)} %pos_ref.1), custom_call_target="tpu_custom_call" | custom-call | flops 9663676416 | bytes 8388608 | tf_op jit(solution)/shard_map/pallas_call | solution.py:576
  71.5 5.5 %shard_map.86 = (f32[3,512,512]{2,1,0:T(8,128)}, f32[512,128]{1,0:T(8,128)}, f32[1,512]{1,0:T(1,128)}) custom-call(f32[3,512,512]{2,1,0:T(8,128)} %bitcast.4, f32[512,128]{1,0:T(8,128)} %get-tuple-element.10.projector, f32[1,512]{1,0:T(1,128)} %get-tuple-element.11.gains), custom_call_target="tpu_custom_call" | custom-call | tf_op jit(solution)/shard_map/pallas_call | solution.py:601

commit v4 on v3

--- a/solution.py
+++ b/solution.py
@@ -19,7 +19,6 @@
 BF16 = jnp.bfloat16
 BLOCK_SEGS = 4
 PARTS = 1
-PLACE_ROWS = 256
 
 
 class Links:
@@ -66,7 +65,7 @@
     head_ref,
     group_ref,
     pos_ref,
-    taps_out,
+    full,
     proj_out,
     gain_out,
     seg_ref,
@@ -87,7 +86,6 @@
     r_a2,
     r_b2,
     r_z,
-    full,
     pacc,
     pwork,
     pr_a1,
@@ -103,7 +101,6 @@
     send_sem,
     recv_sem,
     load_sem,
-    store_sem,
 ):
     n_row, n_grp, n_hi, n_lo, n_z, total_segments = dims
     segs, length, chans = seg_ref.shape
@@ -144,9 +141,13 @@
         part = pl.ds(b * BLOCK_SEGS, BLOCK_SEGS)
         return pltpu.make_async_copy(seg_hbm.at[part], seg_ref.at[part], load_sem.at[b])
 
-    w_load = pltpu.make_async_copy(w_hbm, w_ref, load_sem.at[n_blocks])
+    w_loads = [
+        pltpu.make_async_copy(w_hbm.at[k], w_ref.at[k], load_sem.at[n_blocks + k])
+        for k in range(n_taps)
+    ]
     seg_load(0).start()
-    w_load.start()
+    for load in w_loads:
+        load.start()
     for b in range(1, n_blocks):
         seg_load(b).start()
     group_one = as_column(group_ref[...]).astype(jnp.int32)
@@ -154,47 +155,56 @@
         group_one == lax.broadcasted_iota(jnp.int32, (segs, proj), 1), 1.0, 0.0
     ).astype(F32)
     embeds[row, :, proj:] = hot
-    w_load.wait()
-
-    @pl.loop(0, n_blocks)
-    def _(b):
+
+    def norm_block(b):
         seg_load(b).wait()
-
-        @pl.loop(0, BLOCK_SEGS)
-        def _(i):
+        for i in range(BLOCK_SEGS):
             s = b * BLOCK_SEGS + i
             inputs = seg_ref[s].astype(F32)
             scale = lax.rsqrt(jnp.mean(inputs * inputs, axis=-1, keepdims=True) + EPS)
             normal = inputs * scale
             unit[s] = normal
             normed = normal * gain_ref[...]
-            rows = pl.ds(pl.multiple_of(i * length, length), length)
-            x3[rows, 0:chans] = shift_rows(normed, DILATION_GAP, length).astype(BF16)
-            x3[rows, chans : 2 * chans] = normed.astype(BF16)
-            x3[rows, 2 * chans : 3 * chans] = shift_rows(normed, -DILATION_GAP, length).astype(BF16)
+            rows = slice(i * length, (i + 1) * length)
+            x3[b % 2, rows, 0:chans] = shift_rows(normed, DILATION_GAP, length).astype(BF16)
+            x3[b % 2, rows, chans : 2 * chans] = normed.astype(BF16)
+            x3[b % 2, rows, 2 * chans : 3 * chans] = shift_rows(
+                normed, -DILATION_GAP, length
+            ).astype(BF16)
             n_t[s] = normed.T.astype(BF16)
 
-        conv[...] = jnp.dot(
-            x3[...], w_ref[...].reshape(n_taps * chans, chans), preferred_element_type=F32
+    def conv_block(b):
+        conv[b % 2] = jnp.dot(
+            x3[b % 2], w_ref[...].reshape(n_taps * chans, chans), preferred_element_type=F32
         )
 
-        @pl.loop(0, BLOCK_SEGS)
-        def _(i):
+    def gelu_block(b):
+        for i in range(BLOCK_SEGS):
             s = b * BLOCK_SEGS + i
             total = jnp.zeros((8, chans), F32)
-            step = 32
+            step = 16
             for q in range(length // step):
-                rows = pl.ds(pl.multiple_of(i * length + q * step, step), step)
-                v = conv[rows, :]
+                rows = slice(i * length + q * step, i * length + (q + 1) * step)
+                v = conv[b % 2, rows, :]
                 v2 = v * v
-                th = jnp.tanh(GELU_A * (v + GELU_B * (v2 * v)))
-                cdf = 0.5 * (1.0 + th)
+                th = jnp.tanh(v * (GELU_A + (GELU_A * GELU_B) * v2))
+                cdf = 0.5 + 0.5 * th
                 hidden = seg_ref[s, q * step : (q + 1) * step].astype(F32) + v * cdf
-                dgelu[s, q * step : (q + 1) * step] = cdf + (0.5 * GELU_A) * v * (
-                    1.0 - th * th
-                ) * (1.0 + (3.0 * GELU_B) * v2)
+                slope = (0.5 * GELU_A) + (1.5 * GELU_A * GELU_B) * v2
+                dgelu[s, q * step : (q + 1) * step] = cdf + v * (1.0 - th * th) * slope
                 total = total + hidden.reshape(step // 8, 8, chans).sum(axis=0)
-            pooled[pl.ds(s, 1), :] = jnp.sum(total, axis=0, keepdims=True) * (1.0 / length)
+            pooled[s : s + 1, :] = jnp.sum(total, axis=0, keepdims=True) * (1.0 / length)
+
+    for phase in range(n_blocks + 2):
+        if phase == 1:
+            for load in w_loads:
+                load.wait()
+        if 1 <= phase <= n_blocks:
+            conv_block(phase - 1)
+        if phase < n_blocks:
+            norm_block(phase)
+        if phase >= 2:
+            gelu_block(phase - 2)
 
     pool16 = pooled[...].astype(BF16)
     projected = jnp.dot(pool16, head_ref[...], preferred_element_type=F32)
@@ -368,20 +378,6 @@
         lhs = jnp.concatenate([n_t[s, first : first + part_rows] for s in range(segs)], axis=1)
         put(acc_, side, jnp.dot(lhs, g3[k, side], preferred_element_type=F32))
 
-    stores = []
-
-    def store_tap(c):
-        for side in range(2):
-            for part in range(2):
-                first = side * half + part * quarter
-                store = pltpu.make_async_copy(
-                    full.at[c, side, part],
-                    taps_out.at[c, :, :, :, :, :, pl.ds(first, quarter)],
-                    store_sem.at[len(stores)],
-                )
-                store.start()
-                stores.append(store)
-
     def store_proj():
         for side in range(2):
             for part in range(2):
@@ -406,7 +402,7 @@
     chunks += [
         Chunk(
             functools.partial(fill_tap, c),
-            functools.partial(store_tap, c),
+            lambda: None,
             [buffer.at[c] for buffer in tap_buffers],
         )
         for c in sorted(range(n_taps * parts), key=lambda c: c // parts != n_taps // 2)
@@ -504,14 +500,22 @@
         extras.pop(0)()
     for copy in links.copies:
         copy.wait_send()
-    for store in stores:
-        store.wait()
-
-
-def place_kernel(taps, projector, gains, taps_out, projector_out, gains_out):
-    taps_out[...] = taps[...]
-    projector_out[...] = projector[...]
-    gains_out[...] = gains[...]
+
+
+def place_kernel(full, projector, gains, taps_out, projector_out, gains_out, sems):
+    pairs = [(projector, projector_out), (gains, gains_out)]
+    n_chunks, _, _, n_hi, n_lo, n_z, t, _, quarter = full.shape
+    for c in range(n_chunks):
+        for side in range(2):
+            for part in range(2):
+                first = (2 * side + part) * quarter
+                dst = taps_out.at[c, :, :, :, :, :, pl.ds(first, quarter)]
+                pairs.append((full.at[c, side, part], dst))
+    copies = [pltpu.make_async_copy(*pair, sems.at[i]) for i, pair in enumerate(pairs)]
+    for copy in copies:
+        copy.start()
+    for copy in copies:
+        copy.wait()
 
 
 def body(mesh_sizes, segments, conv_weight, gain, head, group, positive):
@@ -550,8 +554,8 @@
     scratch = [
         pltpu.VMEM(records.shape, BF16),
         pltpu.VMEM(conv_weight.shape, BF16),
-        pltpu.VMEM((BLOCK_SEGS * length, n_taps * chans), BF16),
-        pltpu.VMEM((BLOCK_SEGS * length, chans), F32),
+        pltpu.VMEM((2, BLOCK_SEGS * length, n_taps * chans), BF16),
+        pltpu.VMEM((2, BLOCK_SEGS * length, chans), F32),
         pltpu.VMEM((segs, chans, length), BF16),
         pltpu.VMEM((segs, length, chans), F32),
         pltpu.VMEM((segs, length, chans), F32),
@@ -559,7 +563,7 @@
         pltpu.VMEM((segs, chans), F32),
         pltpu.VMEM((n_taps, 2, rows, half), BF16),
         pltpu.VMEM((n_row, segs, 2 * proj), F32),
-        *chunk_shapes(t, (n_chunks,)),
+        *chunk_shapes(t, (n_chunks,))[:-1],
         *chunk_shapes(tp, ()),
         pltpu.VMEM((2, 8, chans), F32),
         pltpu.VMEM((n_lo, 8, chans), F32),
@@ -567,49 +571,41 @@
         pltpu.VMEM((n_z, 8, chans), F32),
         pltpu.SemaphoreType.DMA((copies,)),
         pltpu.SemaphoreType.DMA((copies,)),
-        pltpu.SemaphoreType.DMA((segs // BLOCK_SEGS + 1,)),
-        pltpu.SemaphoreType.DMA((n_chunks * 4,)),
+        pltpu.SemaphoreType.DMA((segs // BLOCK_SEGS + n_taps,)),
     ]
     vmem = pl.BlockSpec(memory_space=pltpu.VMEM)
-    anywhere = pl.BlockSpec(memory_space=pl.ANY)
+    hbm = pl.BlockSpec(memory_space=pltpu.HBM)
     flops = 3 * 2 * rows * chans * chans * n_taps
     taps, projector, gains = pl.pallas_call(
         functools.partial(kernel, (n_row, n_grp, n_hi, n_lo, n_z, count * n_grp)),
+        out_shape=(
+            pltpu.VMEM((n_chunks, 2, 2, n_hi, n_lo, n_z, t, 8, quarter), F32),
+            pltpu.VMEM((chans, proj), F32),
+            pltpu.VMEM((1, chans), F32),
+        ),
+        in_specs=[hbm] * 2 + [vmem] * 4,
+        out_specs=(vmem, vmem, vmem),
+        scratch_shapes=scratch,
+        compiler_params=pltpu.CompilerParams(
+            collective_id=0, has_side_effects=True, vmem_limit_bytes=52 * 1024 * 1024
+        ),
+        cost_estimate=pl.CostEstimate(
+            flops=flops, bytes_accessed=8 * 1024 * 1024, transcendentals=rows * chans
+        ),
+    )(records, conv_weight, gain[None, :], head, group, positive)
+    taps, projector, gains = pl.pallas_call(
+        place_kernel,
         out_shape=(
             jax.ShapeDtypeStruct((n_chunks, n_hi, n_lo, n_z, t, 8, chans), F32),
             jax.ShapeDtypeStruct((chans, proj), F32),
             jax.ShapeDtypeStruct((1, chans), F32),
         ),
-        in_specs=[anywhere] * 2 + [vmem] * 4,
-        out_specs=(anywhere, vmem, vmem),
-        scratch_shapes=scratch,
-        compiler_params=pltpu.CompilerParams(
-            collective_id=0, has_side_effects=True, vmem_limit_bytes=60 * 1024 * 1024
-        ),
-        cost_estimate=pl.CostEstimate(
-            flops=flops, bytes_accessed=8 * 1024 * 1024, transcendentals=rows * chans
-        ),
-    )(records, conv_weight, gain[None, :], head, group, positive)
-    taps = taps.reshape(n_chunks, shards * t * 8, chans)
+        in_specs=[vmem] * 3,
+        out_specs=(hbm,) * 3,
+        scratch_shapes=[pltpu.SemaphoreType.DMA((4 * n_chunks + 2,))],
+    )(taps, projector, gains)
     rows_each = chans // parts
-    pieces = rows_each // PLACE_ROWS
-    places = (
-        pl.BlockSpec((1, PLACE_ROWS, chans), lambda i: (i // pieces, i % pieces, 0)),
-        pl.BlockSpec((chans, proj), lambda i: (0, 0)),
-        pl.BlockSpec((1, chans), lambda i: (0, 0)),
-    )
-    taps, projector, gains = pl.pallas_call(
-        place_kernel,
-        grid=(n_chunks * pieces,),
-        out_shape=(
-            jax.ShapeDtypeStruct((n_chunks, rows_each, chans), F32),
-            jax.ShapeDtypeStruct((chans, proj), F32),
-            jax.ShapeDtypeStruct((1, chans), F32),
-        ),
-        in_specs=places,
-        out_specs=places,
-        compiler_params=pltpu.CompilerParams(vmem_limit_bytes=60 * 1024 * 1024),
-    )(taps, projector, gains)
+    taps = taps.reshape(n_chunks, shards * t * 8, chans)[:, :rows_each]
     return taps.reshape(n_taps, chans, chans), gains.reshape(chans), projector
 
 

time: 77.2 us -> 74.4 us (0.964)
  Pallas kernels: 76.3 us -> 70.5 us
  local copies, waits for them, and re-layouts: 0 us -> 2.93 us
    pallas_call x1, Pallas kernels: 70.9 us -> 66.6 us  [body(): pl.pallas_call(functools.partial(kernel, (n_row, n_grp, n_hi, n_lo, n_z,...]
    unnamed x0 -> x6, local copies, waits for them, and re-layouts: none -> 2.93 us
    pallas_call x1, Pallas kernels: 5.46 us -> 3.85 us  [body(): pl.pallas_call(place_kernel, out_shape=(jax.ShapeDtypeStruct((n_chunks, n...]
where the time goes in v4:
time: 74.4 us; the launch traced here: 74.2 us
  Pallas kernels  70.5 us (95%)
  local copies, waits for them, and re-layouts  2.93 us (4%)
  between operations  0.81 us (1%)
    pallas_call x1, Pallas kernels, body(): pl.pallas_call(functools.partial(kernel, (n_row, n_grp, n_hi, n_lo, n_z,...  66.6 us
    pallas_call x1, Pallas kernels, body(): pl.pallas_call(place_kernel, out_shape=(jax.ShapeDtypeStruct((n_chunks, n...  3.85 us
    unnamed x6, local copies, waits for them, and re-layouts  2.93 us

profile of v4, /device:TPU:0, one launch (start us, length us, event | category | flops | bytes accessed | tf_op | source)
XLA Modules:
  0.0 74.2 jit_solution(15322163072053573495)
XLA Ops:
  0.6 66.6 %shard_map.85 = (f32[3,2,2,2,2,4,4,8,128]{8,7,6,5,4,3,2,1,0:T(8,128)S(1)}, f32[512,128]{1,0:T(8,128)S(1)}, f32[1,512]{1,0:T(1,128)S(1)}) custom-call(bf16[16,128,512]{2,1,0:T(8,128)(2,1)} %bitcast.5, bf16[3,512,512]{2,1,0:T(8,128)(2,1)} %w_hbm.1, f32[1,512]{1,0:T(1,128)} %bitcast.6, bf16[512,128]{1,0:T(8,128)(2,1)} %head_ref.1, s32[1,16]{1,0:T(1,128)} %group_ref.1, ...), custom_call_target="tpu_custom_call" | custom-call | flops 9663676416 | bytes 8388608 | tf_op jit(solution)/shard_map/pallas_call | solution.py:579
  67.3 0.0 copy-start
  67.3 1.6 %copy-done = f32[3,2,2,2,2,4,4,8,128]{8,7,6,5,4,3,2,1,0:T(8,128)} copy-done((f32[3,2,2,2,2,4,4,8,128]{8,7,6,5,4,3,2,1,0:T(8,128)}, f32[3,2,2,2,2,4,4,8,128]{8,7,6,5,4,3,2,1,0:T(8,128)S(1)}, u32[]{:S(2)}) %copy-start) | copy-done | bytes 3145752
  68.9 0.0 copy-start.1
  68.9 0.7 copy-done.1
  69.6 0.0 copy-start.2
  69.6 0.6 copy-done.2
  70.2 3.8 %shard_map.86 = (f32[3,2,2,4,4,8,512]{6,5,4,3,2,1,0:T(8,128)}, f32[512,128]{1,0:T(8,128)}, f32[1,512]{1,0:T(1,128)}) custom-call(f32[3,2,2,2,2,4,4,8,128]{8,7,6,5,4,3,2,1,0:T(8,128)} %copy-done, f32[512,128]{1,0:T(8,128)} %copy-done.1, f32[1,512]{1,0:T(1,128)} %copy-done.2), custom_call_target="tpu_custom_call" | custom-call | tf_op jit(solution)/shard_map/pallas_call | solution.py:596
Async XLA Ops:
  67.3 1.6 %copy-start = (f32[3,2,2,2,2,4,4,8,128]{8,7,6,5,4,3,2,1,0:T(8,128)}, f32[3,2,2,2,2,4,4,8,128]{8,7,6,5,4,3,2,1,0:T(8,128)S(1)}, u32[]{:S(2)}) copy-start(f32[3,2,2,2,2,4,4,8,128]{8,7,6,5,4,3,2,1,0:T(8,128)S(1)} %get-tuple-element.9.full) | copy-start | bytes 9437188
  68.9 0.7 copy-start.1
  69.6 0.6 copy-start.2

commit v5 on v4

--- a/solution.py
+++ b/solution.py
@@ -18,7 +18,9 @@
 F32 = jnp.float32
 BF16 = jnp.bfloat16
 BLOCK_SEGS = 4
-PARTS = 1
+PARTS = 2
+LAG = 0.55
+EXTRA_FROM, EXTRA_EVERY = 14, 3
 
 
 class Links:
@@ -372,8 +374,13 @@
     parts = acc.shape[0] // n_taps
     part_rows = chans // parts
 
+    shifted = []
+
     def fill_tap(c, acc_, side):
         k, part = c // parts, c % parts
+        if k != n_taps // 2 and not shifted:
+            shift_grads()
+            shifted.append(True)
         first = part * part_rows
         lhs = jnp.concatenate([n_t[s, first : first + part_rows] for s in range(segs)], axis=1)
         put(acc_, side, jnp.dot(lhs, g3[k, side], preferred_element_type=F32))
@@ -487,14 +494,13 @@
     extras += [gain_first, gain_lo, gain_hi, gain_z, gain_end]
 
     n_stages = 9
-    for step in range(n_stages + len(chunks) - 1):
-        for c, chunk in enumerate(chunks):
-            stage = step - c
-            if 0 <= stage < n_stages and (step > 0 or c > 0):
-                getattr(chunk, "stage" + str(stage))()
-        if step == parts:
-            shift_grads()
-        if step >= 3 and extras:
+    order = sorted(
+        (stage + LAG * c, c, stage) for c in range(len(chunks)) for stage in range(n_stages)
+    )
+    for i, (_, c, stage) in enumerate(order):
+        if (c, stage) != (0, 0):
+            getattr(chunks[c], "stage" + str(stage))()
+        if i >= EXTRA_FROM and (i - EXTRA_FROM) % EXTRA_EVERY == 0 and extras:
             extras.pop(0)()
     while extras:
         extras.pop(0)()
@@ -600,9 +606,10 @@
             jax.ShapeDtypeStruct((chans, proj), F32),
             jax.ShapeDtypeStruct((1, chans), F32),
         ),
-        in_specs=[vmem] * 3,
+        in_specs=[pl.BlockSpec(memory_space=pl.ANY)] * 3,
         out_specs=(hbm,) * 3,
         scratch_shapes=[pltpu.SemaphoreType.DMA((4 * n_chunks + 2,))],
+        compiler_params=pltpu.CompilerParams(vmem_limit_bytes=2 * 1024 * 1024),
     )(taps, projector, gains)
     rows_each = chans // parts
     taps = taps.reshape(n_chunks, shards * t * 8, chans)[:, :rows_each]

time: 74.4 us -> 64.4 us (0.87)
  Pallas kernels: 70.5 us -> 63.4 us
  local copies, waits for them, and re-layouts: 2.93 us -> 0 us
    pallas_call x1, Pallas kernels: 66.6 us -> 61.4 us  [body(): pl.pallas_call(functools.partial(kernel, (n_row, n_grp, n_hi, n_lo, n_z,...]
    unnamed x6 -> x0, local copies, waits for them, and re-layouts: 2.93 us -> none
    pallas_call x1, Pallas kernels: 3.85 us -> 1.96 us  [body(): pl.pallas_call(place_kernel, out_shape=(jax.ShapeDtypeStruct((n_chunks, n...]
where the time goes in v5:
time: 64.4 us; the launch traced here: 64.2 us
  Pallas kernels  63.4 us (98%)
  between operations  0.8 us (1%)
    pallas_call x1, Pallas kernels, body(): pl.pallas_call(functools.partial(kernel, (n_row, n_grp, n_hi, n_lo, n_z,...  61.4 us
    pallas_call x1, Pallas kernels, body(): pl.pallas_call(place_kernel, out_shape=(jax.ShapeDtypeStruct((n_chunks, n...  1.96 us

profile of v5, /device:TPU:0, one launch (start us, length us, event | category | flops | bytes accessed | tf_op | source)
XLA Modules:
  0.0 64.2 jit_solution(15606170373566994548)
XLA Ops:
  0.6 61.4 %shard_map.85 = (f32[6,2,2,2,2,4,2,8,128]{8,7,6,5,4,3,2,1,0:T(8,128)S(1)}, f32[512,128]{1,0:T(8,128)S(1)}, f32[1,512]{1,0:T(1,128)S(1)}) custom-call(bf16[16,128,512]{2,1,0:T(8,128)(2,1)} %bitcast.5, bf16[3,512,512]{2,1,0:T(8,128)(2,1)} %w_hbm.1, f32[1,512]{1,0:T(1,128)} %bitcast.6, bf16[512,128]{1,0:T(8,128)(2,1)} %head_ref.1, s32[1,16]{1,0:T(1,128)} %group_ref.1, ...), custom_call_target="tpu_custom_call" | custom-call | flops 9663676416 | bytes 8388608 | tf_op jit(solution)/shard_map/pallas_call | solution.py:585
  62.0 2.0 %shard_map.86 = (f32[6,2,2,4,2,8,512]{6,5,4,3,2,1,0:T(8,128)}, f32[512,128]{1,0:T(8,128)}, f32[1,512]{1,0:T(1,128)}) custom-call(f32[6,2,2,2,2,4,2,8,128]{8,7,6,5,4,3,2,1,0:T(8,128)S(1)} %get-tuple-element.9.full, f32[512,128]{1,0:T(8,128)S(1)} %get-tuple-element.10.projector, f32[1,512]{1,0:T(1,128)S(1)} %get-tuple-element.11.gains), custom_call_target="tpu_custom_call" | custom-call | tf_op jit(solution)/shard_map/pallas_call | solution.py:602

commit v6 on v5

--- a/solution.py
+++ b/solution.py
@@ -19,7 +19,7 @@
 BF16 = jnp.bfloat16
 BLOCK_SEGS = 4
 PARTS = 2
-LAG = 0.55
+LAG = 0.6
 EXTRA_FROM, EXTRA_EVERY = 14, 3
 
 
@@ -392,21 +392,26 @@
                 block_t = pfull[side, part].reshape(-1, quarter)[:proj]
                 proj_out[first : first + quarter, :] = block_t.T
 
-    pool32 = pool16.astype(F32)
-    proj_t = lax.dot_general(
-        projected_grad,
-        pool32,
-        (((0,), (0,)), ((), ())),
-        precision=HIGHEST,
-        preferred_element_type=F32,
-    )
-    for side in range(2):
-        put(pacc, side, proj_t[:, side * half : (side + 1) * half])
+    filled = []
+
+    def fill_proj(acc_, side):
+        if filled:
+            return
+        filled.append(True)
+        pool32 = pool16.astype(F32)
+        proj_t = lax.dot_general(
+            projected_grad,
+            pool32,
+            (((0,), (0,)), ((), ())),
+            precision=HIGHEST,
+            preferred_element_type=F32,
+        )
+        for side in range(2):
+            put(pacc, side, proj_t[:, side * half : (side + 1) * half])
 
     proj_buffers = (pacc, pwork, pr_a1, pr_b1, pr_a2, pr_b2, pr_z, pfull)
     tap_buffers = (acc, work, r_a1, r_b1, r_a2, r_b2, r_z, full)
-    chunks = [Chunk(lambda acc_, side: None, store_proj, proj_buffers)]
-    chunks += [
+    chunks = [
         Chunk(
             functools.partial(fill_tap, c),
             lambda: None,
@@ -414,11 +419,11 @@
         )
         for c in sorted(range(n_taps * parts), key=lambda c: c // parts != n_taps // 2)
     ]
-    chunks[0].stage0()
+    chunks.append(Chunk(fill_proj, store_proj, proj_buffers))
 
     middle = n_taps // 2
 
-    @pl.loop(0, segs)
+    @pl.loop(0, segs, unroll=4)
     def _(s):
         grad = (dgelu[s] * hgrad[pl.ds(s, 1), :]).astype(BF16)
         rows = pl.ds(pl.multiple_of(s * length, length), length)
@@ -426,7 +431,7 @@
             g3[middle, side, rows, :] = grad[:, side * half : (side + 1) * half]
 
     def shift_grads():
-        @pl.loop(0, segs)
+        @pl.loop(0, segs, unroll=2)
         def _(s):
             rows = pl.ds(pl.multiple_of(s * length, length), length)
             for side in range(2):
@@ -498,8 +503,7 @@
         (stage + LAG * c, c, stage) for c in range(len(chunks)) for stage in range(n_stages)
     )
     for i, (_, c, stage) in enumerate(order):
-        if (c, stage) != (0, 0):
-            getattr(chunks[c], "stage" + str(stage))()
+        getattr(chunks[c], "stage" + str(stage))()
         if i >= EXTRA_FROM and (i - EXTRA_FROM) % EXTRA_EVERY == 0 and extras:
             extras.pop(0)()
     while extras:

time: 64.4 us -> 66.8 us (1.037)
  Pallas kernels: 63.4 us -> 65.6 us
    pallas_call x1, Pallas kernels: 61.4 us -> 63.6 us  [body(): pl.pallas_call(functools.partial(kernel, (n_row, n_grp, n_hi, n_lo, n_z,...]
where the time goes in v6:
time: 66.8 us; the launch traced here: 66.4 us
  Pallas kernels  65.6 us (98%)
  between operations  0.8 us (1%)
    pallas_call x1, Pallas kernels, body(): pl.pallas_call(functools.partial(kernel, (n_row, n_grp, n_hi, n_lo, n_z,...  63.6 us
    pallas_call x1, Pallas kernels, body(): pl.pallas_call(place_kernel, out_shape=(jax.ShapeDtypeStruct((n_chunks, n...  1.96 us

profile of v6, /device:TPU:0, one launch (start us, length us, event | category | flops | bytes accessed | tf_op | source)
XLA Modules:
  0.0 66.4 jit_solution(3122154344113954860)
XLA Ops:
  0.6 63.6 %shard_map.85 = (f32[6,2,2,2,2,4,2,8,128]{8,7,6,5,4,3,2,1,0:T(8,128)S(1)}, f32[512,128]{1,0:T(8,128)S(1)}, f32[1,512]{1,0:T(1,128)S(1)}) custom-call(bf16[16,128,512]{2,1,0:T(8,128)(2,1)} %bitcast.5, bf16[3,512,512]{2,1,0:T(8,128)(2,1)} %w_hbm.1, f32[1,512]{1,0:T(1,128)} %bitcast.6, bf16[512,128]{1,0:T(8,128)(2,1)} %head_ref.1, s32[1,16]{1,0:T(1,128)} %group_ref.1, ...), custom_call_target="tpu_custom_call" | custom-call | flops 9663676416 | bytes 8388608 | tf_op jit(solution)/shard_map/pallas_call | solution.py:589
  64.3 2.0 %shard_map.86 = (f32[6,2,2,4,2,8,512]{6,5,4,3,2,1,0:T(8,128)}, f32[512,128]{1,0:T(8,128)}, f32[1,512]{1,0:T(1,128)}) custom-call(f32[6,2,2,2,2,4,2,8,128]{8,7,6,5,4,3,2,1,0:T(8,128)S(1)} %get-tuple-element.9.full, f32[512,128]{1,0:T(8,128)S(1)} %get-tuple-element.10.projector, f32[1,512]{1,0:T(1,128)S(1)} %get-tuple-element.11.gains), custom_call_target="tpu_custom_call" | custom-call | tf_op jit(solution)/shard_map/pallas_call | solution.py:606
